TPU v7x, 512 devices: a whole 4x8x8 slice. The times are simulated.
512 devices in a mesh: fsdp: 64 (over z, y_hi, core), replica: 8 (over y_lo, x).
Axes of the slice: x: 4, y: 8 (y_hi: 4, y_lo: 2; y = y_hi * 2 + y_lo), z: 8, core: 2. Of those that a mesh axis runs over, the one named last changes fastest.
Arguments:
- weights: bfloat16 [4096, 14336], P('fsdp'), may hold values from -5 to 5
- momentum: float32 [4096, 14336], P('fsdp', 'replica'), may hold values from -3 to 3
- hidden: bfloat16 [8, 7, 64, 14336], P('replica', None, 'fsdp'), may hold values from -8 to 8, as said below
- targets: bfloat16 [8, 7, 64, 4096], P('replica', None, None, 'fsdp'), may hold values from -24 to 24
Outputs:
- new_weights: bfloat16 [8, 4096, 14336], P('replica', 'fsdp')
- outer_weights: bfloat16 [4096, 14336], P('fsdp', 'replica')
- momentum_out: float32 [4096, 14336], P('fsdp', 'replica')
Inputs may be any that keep to these rules, and one draw needn't show every extreme that they name: `hidden`: hidden activations of the layer.
All inputs are finite; a program needn't handle non-finite values.
Results may differ from a plain program's by a relative error of at most 0.013.
Values may be sent and summed in bfloat16 or wider, within the bound.
No kernel may reach another device: no remote copies, remote signals or barrier semaphores. Data moves between devices by JAX's collectives and lax.ppermute only.
A program may use at most 128 MiB of HBM per device.

v0:
```python
import math

import jax
import jax.numpy as jnp
from jax import lax
from jax.sharding import PartitionSpec as P

BEFORE = 3
DURING = 4


inner_rate = 0.4
outer_rate = 0.7
momentum_rate = 0.9
mixing = 0.5


def synchronize(weights, momentum, early_weights):
    groups = lax.axis_size("replica")
    group_index = lax.axis_index("replica")
    columns = weights.shape[1]
    shard_width = columns // groups
    pseudo = weights.astype(jnp.float32) - early_weights.astype(jnp.float32)
    encoded = pseudo.astype(jnp.bfloat16)
    summed = lax.psum_scatter(
        encoded.astype(jnp.float32).astype(jnp.bfloat16), "replica", scatter_dimension=1, tiled=True
    ).astype(jnp.float32)
    average = summed / groups
    momentum_out = momentum_rate * momentum + average
    start_rows = lax.dynamic_slice_in_dim(
        weights, group_index * shard_width, shard_width, 1
    ).astype(jnp.float32)
    outer_shard = (start_rows - outer_rate * (average + momentum_rate * momentum_out)).astype(
        jnp.bfloat16
    )
    outer_full = lax.all_gather(outer_shard, "replica", axis=1, tiled=True)
    return (outer_shard, momentum_out, outer_full)


def body(weights, momentum, hidden, targets):
    inverse_root = 1.0 / math.sqrt(weights.shape[1])

    def tokens_of(number):
        return lax.all_gather(hidden[0, number], "fsdp", axis=0, tiled=True)

    def advance(current, number):
        hidden_rows = tokens_of(number)
        projected = (
            lax.dot_general(
                hidden_rows, current, (((1,), (1,)), ((), ())), preferred_element_type=jnp.float32
            )
            * inverse_root
        )
        residual = (projected - targets[0, number].astype(jnp.float32)).astype(jnp.bfloat16)
        update = lax.dot_general(
            residual, hidden_rows, (((0,), (0,)), ((), ())), preferred_element_type=jnp.float32
        )
        return (current.astype(jnp.float32) - inner_rate * inverse_root * update).astype(
            jnp.bfloat16
        )

    current = weights
    for number in range(BEFORE):
        current = advance(current, number)
    early_weights = current
    for number in range(BEFORE, BEFORE + DURING):
        current = advance(current, number)
    outer_shard, momentum_out, outer_full = synchronize(weights, momentum, early_weights)
    mixed = mixing * current.astype(jnp.float32) + (1.0 - mixing) * outer_full.astype(jnp.float32)
    new_weights = mixed.astype(jnp.bfloat16)[None]
    return (new_weights, outer_shard, momentum_out)


def solution(mesh):
    placed = (
        P("fsdp", None),
        P("fsdp", "replica"),
        P("replica", None, "fsdp", None),
        P("replica", None, None, "fsdp"),
    )
    return jax.shard_map(
        body,
        mesh=mesh,
        in_specs=placed,
        out_specs=(P("replica", "fsdp", None), P("fsdp", "replica"), P("fsdp", "replica")),
        check_vma=False,
    )
```

profile of v0, /device:TPU:1, one launch (start us, length us, event | category | flops | bytes accessed | tf_op | source)
XLA Modules:
  0.0 730.2 jit_solution(13690312257739353121)
XLA Ops:
  7.2 3.0 slice_bitcast_fusion
  10.3 0.7 all-gather.20.cloned.1.call-update
  11.0 0.7 all-gather.22.cloned.1.call-update
  11.8 0.8 fusion.179
  12.8 91.1 %all-gather.18.cloned.1.call-done = bf16[64,1,1,14336]{3,2,1,0:T(2,128)(2,1)} async-done(((bf16[1,1,1,14336]{3,2,1,0:T(2,128)(2,1)}), bf16[64,1,1,14336]{3,2,1,0:T(2,128)(2,1)}) %all-gather.18.cloned.1.call-update) | async-done | bytes 1835024 | tf_op jit(solution)/shard_map/all_gather | solution.py:44
  103.9 8.4 %fusion.17 = bf16[64,14336]{1,0:T(8,128)(2,1)} fusion(bf16[64,14336]{1,0:T(8,128)(2,1)} %param.4, bf16[64,1,1,14336]{3,2,1,0:T(2,128)(2,1)} %all-gather.18.cloned.1.call-done, bf16[1,7,64,64]{3,2,1,0:T(8,128)(2,1)} %param.7), kind=kOutput, calls=%fused_computation.24 | convolution fusion | flops 238567424 | bytes 12861440 | tf_op jit(solution)/shard_map/dot_general | solution.py:55
  112.3 78.2 %all-gather.20.cloned.1.call-done = bf16[64,1,1,14336]{3,2,1,0:T(2,128)(2,1)} async-done(((bf16[1,1,1,14336]{3,2,1,0:T(2,128)(2,1)}), bf16[64,1,1,14336]{3,2,1,0:T(2,128)(2,1)}) %all-gather.20.cloned.1.call-update) | async-done | bytes 1835024 | tf_op jit(solution)/shard_map/all_gather | solution.py:44
  190.5 8.2 %fusion.16 = bf16[64,14336]{1,0:T(8,128)(2,1)} fusion(bf16[64,14336]{1,0:T(8,128)(2,1)} %fusion.17, bf16[64,1,1,14336]{3,2,1,0:T(2,128)(2,1)} %all-gather.20.cloned.1.call-done, bf16[1,1,64,64]{2,3,1,0:T(8,128)(2,1)S(1)} %copy.38), kind=kOutput, calls=%fused_computation.23 | convolution fusion | flops 238567424 | bytes 5513216 | tf_op jit(solution)/shard_map/dot_general | solution.py:55
  198.7 78.5 %all-gather.22.cloned.1.call-done = bf16[64,1,1,14336]{3,2,1,0:T(2,128)(2,1)} async-done(((bf16[1,1,1,14336]{3,2,1,0:T(2,128)(2,1)}), bf16[64,1,1,14336]{3,2,1,0:T(2,128)(2,1)}) %all-gather.22.cloned.1.call-update) | async-done | bytes 1835024 | tf_op jit(solution)/shard_map/all_gather | solution.py:44
  277.2 8.9 %fusion.19 = (bf16[64,14336]{1,0:T(8,128)(2,1)}, bf16[64,14336]{1,0:T(8,128)(2,1)}) fusion(bf16[64,14336]{1,0:T(8,128)(2,1)S(1)} %copy-done, bf16[64,1,1,14336]{3,2,1,0:T(2,128)(2,1)} %all-gather.22.cloned.1.call-done, bf16[64,14336]{1,0:T(8,128)(2,1)} %fusion.16, bf16[1,1,64,64]{2,3,1,0:T(8,128)(2,1)S(1)} %copy.40), kind=kOutput, calls=%fused_computation.27 | convolution fusion | flops 242237440 | bytes 9183232 | tf_op jit(solution)/shard_map/dot_general | solution.py:55
  286.2 0.5 all-gather.24.cloned.1.call-update
  287.3 0.7 all-gather.28.cloned.1.call-update
  288.1 0.7 all-gather.30.cloned.1.call-update
  289.0 35.8 %reduce-scatter.2.cloned.1.call-done = bf16[64,1792]{1,0:T(8,128)(2,1)} async-done(((bf16[64,14336]{1,0:T(8,128)(2,1)}), bf16[64,1792]{1,0:T(8,128)(2,1)}) %reduce-scatter.2.cloned.1.call-update) | async-done | bytes 229392 | tf_op jit(solution)/shard_map/reduce_scatter | solution.py:25
  324.8 1.9 subtract_convert_fusion
  327.1 91.1 %all-gather.24.cloned.1.call-done = bf16[64,1,1,14336]{3,2,1,0:T(2,128)(2,1)} async-done(((bf16[1,1,1,14336]{3,2,1,0:T(2,128)(2,1)}), bf16[64,1,1,14336]{3,2,1,0:T(2,128)(2,1)}) %all-gather.24.cloned.1.call-update) | async-done | bytes 1835024 | tf_op jit(solution)/shard_map/all_gather | solution.py:44
  418.2 6.9 fusion.14
  425.1 79.0 %all-gather.26.cloned.1.call-done = bf16[64,1,1,14336]{3,2,1,0:T(2,128)(2,1)} async-done(((bf16[1,1,1,14336]{3,2,1,0:T(2,128)(2,1)}), bf16[64,1,1,14336]{3,2,1,0:T(2,128)(2,1)}) %all-gather.26.cloned.1.call-update) | async-done | bytes 1835024 | tf_op jit(solution)/shard_map/all_gather | solution.py:44
  504.2 7.1 fusion.13
  511.3 79.0 %all-gather.28.cloned.1.call-done = bf16[64,1,1,14336]{3,2,1,0:T(2,128)(2,1)} async-done(((bf16[1,1,1,14336]{3,2,1,0:T(2,128)(2,1)}), bf16[64,1,1,14336]{3,2,1,0:T(2,128)(2,1)}) %all-gather.28.cloned.1.call-update) | async-done | bytes 1835024 | tf_op jit(solution)/shard_map/all_gather | solution.py:44
  590.2 6.9 fusion.12
  597.1 79.2 %all-gather.30.cloned.1.call-done = bf16[64,1,1,14336]{3,2,1,0:T(2,128)(2,1)} async-done(((bf16[1,1,1,14336]{3,2,1,0:T(2,128)(2,1)}), bf16[64,1,1,14336]{3,2,1,0:T(2,128)(2,1)}) %all-gather.30.cloned.1.call-update) | async-done | bytes 1835024 | tf_op jit(solution)/shard_map/all_gather | solution.py:44
  676.3 39.6 %all-gather.16.cloned.1.call-done = bf16[64,14336]{1,0:T(8,128)(2,1)} async-done(((bf16[64,1792]{1,0:T(8,128)(2,1)}), bf16[64,14336]{1,0:T(8,128)(2,1)}) %all-gather.16.cloned.1.call-update) | async-done | bytes 1835024 | tf_op jit(solution)/shard_map/all_gather | solution.py:36
  715.9 7.7 %fusion.18 = bf16[1,64,14336]{2,1,0:T(8,128)(2,1)} fusion(bf16[64,14336]{1,0:T(8,128)(2,1)} %all-gather.16.cloned.1.call-done, bf16[64,14336]{1,0:T(8,128)(2,1)S(1)} %fusion.12, bf16[64,1,1,14336]{3,2,1,0:T(2,128)(2,1)} %all-gather.30.cloned.1.call-done, bf16[1,1,64,64]{2,3,1,0:T(8,128)(2,1)S(1)} %copy.48), kind=kOutput, calls=%fused_computation.25 | convolution fusion | flops 243154944 | bytes 7348224 | tf_op jit(solution)/shard_map/dot_general | solution.py:55
  (23 shorter events, 1.7 us)
Async XLA Ops:
  7.2 96.7 %all-gather.18.cloned.1.call-start = ((), (), s32[]{:S(2)}) async-start(), calls=%async_computation.3 | async-start | bytes 3727360 | tf_op jit(solution)/shard_map/all_gather | solution.py:44
  10.2 180.3 %all-gather.20.cloned.1.call-start = ((), (), s32[]{:S(2)}) async-start(), calls=%async_computation.4 | async-start | bytes 3727360 | tf_op jit(solution)/shard_map/all_gather | solution.py:44
  11.0 266.2 %all-gather.22.cloned.1.call-start = ((), (), s32[]{:S(2)}) async-start(), calls=%async_computation.5 | async-start | bytes 3727360 | tf_op jit(solution)/shard_map/all_gather | solution.py:44
  11.7 313.1 %reduce-scatter.2.cloned.1.call-start = ((), (), s32[]{:S(2)}) async-start(), calls=%async_computation.1 | async-start | bytes 2064384 | tf_op jit(solution)/shard_map/reduce_scatter | solution.py:25
  112.3 164.9 %copy-start = (bf16[64,14336]{1,0:T(8,128)(2,1)S(1)}, bf16[64,14336]{1,0:T(8,128)(2,1)}, u32[]{:S(2)}) copy-start(bf16[64,14336]{1,0:T(8,128)(2,1)} %param.4) | copy-start | bytes 5505028
  198.7 126.1 %copy-start.1 = (f32[64,1792]{1,0:T(8,128)S(1)}, f32[64,1792]{1,0:T(8,128)}, u32[]{:S(2)}) copy-start(f32[64,1792]{1,0:T(8,128)} %param.5) | copy-start | bytes 1376260
  286.1 132.1 %all-gather.24.cloned.1.call-start = ((), (), s32[]{:S(2)}) async-start(), calls=%async_computation.6 | async-start | bytes 3727360 | tf_op jit(solution)/shard_map/all_gather | solution.py:44
  286.7 217.4 %all-gather.26.cloned.1.call-start = ((), (), s32[]{:S(2)}) async-start(), calls=%async_computation.7 | async-start | bytes 3727360 | tf_op jit(solution)/shard_map/all_gather | solution.py:44
  287.3 302.9 %all-gather.28.cloned.1.call-start = ((), (), s32[]{:S(2)}) async-start(), calls=%async_computation.8 | async-start | bytes 3727360 | tf_op jit(solution)/shard_map/all_gather | solution.py:44
  288.0 388.3 %all-gather.30.cloned.1.call-start = ((), (), s32[]{:S(2)}) async-start(), calls=%async_computation.9 | async-start | bytes 3727360 | tf_op jit(solution)/shard_map/all_gather | solution.py:44
  288.8 427.1 %all-gather.16.cloned.1.call-start = ((), (), s32[]{:S(2)}) async-start(), calls=%async_computation.2 | async-start | bytes 2064384 | tf_op jit(solution)/shard_map/all_gather | solution.py:36
Sparse Core Ops, SparseCore 0:
  11.9 91.9 all-gather.17
  107.8 82.7 all-gather.19
  194.4 82.7 all-gather.21
  286.3 38.5 reduce-scatter.1
  328.0 90.1 all-gather.23
  421.4 82.7 all-gather.25
  507.5 82.7 all-gather.27
  593.6 82.7 all-gather.29
  679.0 36.8 all-gather.15
where the time goes:
time: 735 us; the launch traced here: 730 us
  waiting for transfers between devices  655 us (89%)
  matrix products  54.2 us (7%)
  between operations  13.9 us (2%)
    all_gather x7, waiting for transfers between devices, tokens_of(): return lax.all_gather(hidden[0, number], 'fsdp', axis=0, tiled=True)  576 us
    dot_general x7, matrix products, advance(): lax.dot_general(residual, hidden_rows, (((0,), (0,)), ((), ())), preferre...  54.2 us
    all_gather x1, waiting for transfers between devices, synchronize(): outer_full = lax.all_gather(outer_shard, 'replica', axis=1, tiled=True)  39.6 us
    reduce_scatter x1, waiting for transfers between devices, synchronize(): lax.psum_scatter(encoded.astype(jnp.float32).astype(jnp.bfloat16), 'repli...  35.8 us
  transfers between devices with their start and end apart: 9, of which 9 were waited for; matrix products, arithmetic and copies ran while one was open for 6% of the time, Pallas kernels for 0%

commit v1 on v0

v1 whole, which is shorter than its diff:
```python
import functools
import math

import jax
import jax.numpy as jnp
from jax import lax
from jax.experimental import pallas as pl
from jax.experimental.pallas import tpu as pltpu
from jax.sharding import Mesh
from jax.sharding import PartitionSpec as P

BEFORE = 3
DURING = 4

inner_rate = 0.4
outer_rate = 0.7
momentum_rate = 0.9
mixing = 0.5

PIECES = 8
MESH_AXES = ("z", "y", "core", "y_lo", "x")
FSDP = ("z", "y", "core")
REPLICA = ("y_lo", "x")
VMEM_LIMIT = 48 * 1024 * 1024


def window_kernel(steps, early, *refs):
    if early:
        hidden, weights, targets, out, hs, ws, outs, hidden_sem, weights_sem, out_sem = refs
    else:
        (hidden, weights, encoded, targets, out, hs, ws, es, outs, hidden_sem, weights_sem,
         encoded_sem, out_sem) = refs
    rows = hidden.shape[0]
    width = hs.shape[2]
    features = ws.shape[1]
    inverse_root = 1.0 / math.sqrt(width * PIECES)

    def columns(piece):
        return pl.ds(piece * width, width)

    def hidden_copy(piece):
        return pltpu.make_async_copy(
            hidden.at[:, columns(piece)], hs.at[piece], hidden_sem.at[piece])

    def weights_copy(piece):
        return pltpu.make_async_copy(
            weights.at[:, columns(piece)], ws.at[piece], weights_sem.at[piece])

    def encoded_copy(piece):
        return pltpu.make_async_copy(encoded.at[piece], es.at[piece], encoded_sem.at[piece])

    def out_copy(piece):
        target = out.at[piece] if early else out.at[:, columns(piece)]
        return pltpu.make_async_copy(outs.at[piece], target, out_sem.at[piece])

    for piece in range(PIECES):
        hidden_copy(piece).start()
        weights_copy(piece).start()
        if not early:
            encoded_copy(piece).start()

    across = (((1,), (1,)), ((), ()))

    def gather_products(piece, carry):
        projected, gram = carry
        weights_copy(piece).wait()
        current = ws[piece]
        if not early:
            encoded_copy(piece).wait()
            current = (current.astype(jnp.float32) - es[piece].astype(jnp.float32)).astype(
                jnp.bfloat16)
            ws[piece] = current
        hidden_copy(piece).wait()
        block = hs[piece]
        projected += lax.dot_general(block, current, across, preferred_element_type=jnp.float32)
        gram += lax.dot_general(block, block, across, preferred_element_type=jnp.float32)
        return projected, gram

    projected, gram = lax.fori_loop(
        0, PIECES, gather_products,
        (jnp.zeros((rows, features), jnp.float32), jnp.zeros((rows, rows), jnp.float32)))

    gram_high = gram.astype(jnp.bfloat16)
    gram_low = (gram - gram_high.astype(jnp.float32)).astype(jnp.bfloat16)
    step_of = lax.broadcasted_iota(jnp.int32, (rows, features), 0) % steps
    wanted = targets[...].astype(jnp.float32)
    scaled = projected * inverse_root
    residual = jnp.zeros((rows, features), jnp.float32)
    for number in range(steps):
        moved = scaled
        if number:
            short = residual.astype(jnp.bfloat16)
            product = jnp.dot(gram_high, short, preferred_element_type=jnp.float32)
            product += jnp.dot(gram_low, short, preferred_element_type=jnp.float32)
            moved = scaled - (inner_rate * inverse_root * inverse_root) * product
        fresh = (moved - wanted).astype(jnp.bfloat16).astype(jnp.float32)
        residual = jnp.where(step_of == number, fresh, residual)
    turned = residual.T.astype(jnp.bfloat16)

    def write(piece, carry):
        update = (inner_rate * inverse_root) * jnp.dot(
            turned, hs[piece], preferred_element_type=jnp.float32)
        if early:
            outs[piece] = update.astype(jnp.bfloat16)
        else:
            outs[piece] = (ws[piece].astype(jnp.float32) - update).astype(jnp.bfloat16)
        out_copy(piece).start()
        return carry

    lax.fori_loop(0, PIECES, write, 0)
    for piece in range(PIECES):
        out_copy(piece).wait()


def run_window(steps, hidden, weights, targets, encoded=None):
    early = encoded is None
    rows = hidden.shape[0]
    features, columns = weights.shape
    width = columns // PIECES
    anywhere = pl.BlockSpec(memory_space=pl.ANY)
    whole = pl.BlockSpec(memory_space=pltpu.VMEM)
    held = pltpu.VMEM((PIECES, features, width), jnp.bfloat16)
    semaphores = pltpu.SemaphoreType.DMA((PIECES,))
    count = 1 if early else 2
    operands = (hidden, weights, targets) if early else (hidden, weights, encoded, targets)
    return pl.pallas_call(
        functools.partial(window_kernel, steps, early),
        out_shape=jax.ShapeDtypeStruct(
            (PIECES, features, width) if early else (features, columns), jnp.bfloat16),
        in_specs=[anywhere] * (1 + count) + [whole],
        out_specs=anywhere,
        scratch_shapes=[pltpu.VMEM((PIECES, rows, width), jnp.bfloat16)]
        + [held] * (1 + count) + [semaphores] * (2 + count),
        compiler_params=pltpu.CompilerParams(vmem_limit_bytes=VMEM_LIMIT),
        cost_estimate=pl.CostEstimate(
            flops=2 * rows * columns * (rows + 2 * features),
            bytes_accessed=2 * columns * (rows + (2 + count) * features), transcendentals=0),
        name="early_window" if early else "late_window",
    )(*operands)


def mix_kernel(late, outer, out):
    out[...] = (
        mixing * late[...].astype(jnp.float32) + (1.0 - mixing) * outer[...].astype(jnp.float32)
    ).astype(jnp.bfloat16)


def mix(late, outer):
    features, columns = late.shape
    width = columns // PIECES
    flat = pl.BlockSpec((features, width), lambda piece: (0, piece))
    return pl.pallas_call(
        mix_kernel,
        grid=(PIECES,),
        out_shape=jax.ShapeDtypeStruct((features, columns), jnp.bfloat16),
        in_specs=[flat, pl.BlockSpec((None, features, width), lambda piece: (piece, 0, 0))],
        out_specs=flat,
        cost_estimate=pl.CostEstimate(
            flops=3 * features * columns, bytes_accessed=6 * features * columns,
            transcendentals=0),
        name="mix",
    )(late, outer)


def body(weights, momentum, hidden, targets):
    features, columns = weights.shape
    width = columns // PIECES
    groups = lax.axis_size(REPLICA)
    lanes = lax.axis_size("y")
    outer_ring = lax.axis_size(("z", "core"))
    own = hidden.reshape(BEFORE + DURING, PIECES, width)

    def gathered(part, steps):
        near = lax.all_gather(part.reshape(steps * PIECES, width), "y", axis=0, tiled=True)
        if steps * lanes % 8 == 0:
            near = near.reshape(lanes * steps, columns)
        far = lax.all_gather(near, ("z", "core"), axis=0, tiled=True)
        return far.reshape(outer_ring * lanes * steps, columns)

    def target_rows(part, steps):
        parts = part.reshape(steps, lax.axis_size("z"), lanes, lax.axis_size("core"), features)
        return parts.transpose(1, 3, 2, 0, 4).reshape(-1, features)

    early_hidden = gathered(own[:BEFORE], BEFORE)
    late_hidden = gathered(own[BEFORE:], DURING)
    early_targets = target_rows(targets[0, :BEFORE], BEFORE)
    late_targets = target_rows(targets[0, BEFORE:], DURING)

    encoded = run_window(BEFORE, early_hidden, weights, early_targets)
    received = lax.all_to_all(encoded, REPLICA, split_axis=0, concat_axis=0, tiled=True)
    average = jnp.sum(received.astype(jnp.float32), axis=0) / groups
    momentum_out = momentum_rate * momentum + average
    start_rows = lax.dynamic_slice_in_dim(
        weights, lax.axis_index(REPLICA) * width, width, 1
    ).astype(jnp.float32)
    outer_shard = (start_rows - outer_rate * (average + momentum_rate * momentum_out)).astype(
        jnp.bfloat16
    )
    outer_full = lax.all_to_all(
        jnp.broadcast_to(outer_shard, (groups, features, width)),
        REPLICA, split_axis=0, concat_axis=0, tiled=True)

    late = run_window(DURING, late_hidden, weights, late_targets, encoded)
    new_weights = mix(late, outer_full)[None]
    return (new_weights, outer_shard, momentum_out)


def solution(mesh):
    fine = Mesh(mesh.devices.reshape(8, 4, 2, 2, 4), MESH_AXES)
    placed = (
        P(FSDP, None),
        P(FSDP, REPLICA),
        P(REPLICA, None, FSDP, None),
        P(REPLICA, None, None, FSDP),
    )
    return jax.shard_map(
        body,
        mesh=fine,
        in_specs=placed,
        out_specs=(P(REPLICA, FSDP, None), P(FSDP, REPLICA), P(FSDP, REPLICA)),
        check_vma=False,
    )
```

time: 735 us -> 169 us (0.23)
  waiting for transfers between devices: 655 us -> 72.8 us
  matrix products: 54.2 us -> 0 us
  blocking collectives: 0 us -> 29.3 us
  Pallas kernels: 0 us -> 26 us
  local copies, waits for them, and re-layouts: 4.38 us -> 14.2 us
  starting transfers between devices: 0.53 us -> 9.45 us
    all_gather x8 -> x2, waiting for transfers between devices: 616 us -> 38.3 us  [gathered(): far = lax.all_gather(near, ('z', 'core'), axis=0, tiled=True)]
    dot_general x7 -> x0, matrix products: 54.2 us -> none  [advance(): lax.dot_general(residual, hidden_rows, (((0,), (0,)), ((), ())), preferre...]
    reduce_scatter x1 -> x0, waiting for transfers between devices: 35.8 us -> none  [synchronize(): lax.psum_scatter(encoded.astype(jnp.float32).astype(jnp.bfloat16), 'repli...]
    all_to_all x0 -> x2, waiting for transfers between devices: none -> 34.4 us  [the longest x1 23.5 us: body(): lax.all_to_all(encoded, REPLICA, split_axis=0, concat_axis=0, tiled=True)]
    all_gather x0 -> x2, blocking collectives: none -> 29.3 us  [gathered(): lax.all_gather(part.reshape(steps * PIECES, width), 'y', axis=0, tiled=True)]
    pallas_call x0 -> x3, Pallas kernels: none -> 26 us  [the longest x2 19.7 us: run_window(): pl.pallas_call(functools.partial(window_kernel, steps, early), out_shape=...]
    reshape x0 -> x5, local copies, waits for them, and re-layouts: none -> 9.46 us  [the longest x1 8.27 us: gathered(): return far.reshape(outer_ring * lanes * steps, columns)]
    all_to_all x0 -> x2, starting transfers between devices: none -> 9.37 us  [the longest x1 4.92 us: body(): lax.all_to_all(encoded, REPLICA, split_axis=0, concat_axis=0, tiled=True)]
  transfers between devices with their start and end apart: 9 -> 4, of which waited for: 9 -> 4; matrix products, arithmetic and copies ran while one was open for 6% -> 9% of each run, Pallas kernels for 0% -> 12%
where the time goes in v1:
time: 169 us
  waiting for transfers between devices  72.8 us (43%)
  blocking collectives  29.3 us (17%)
  Pallas kernels  26 us (15%)
  local copies, waits for them, and re-layouts  14.2 us (8%)
  between operations  14.2 us (8%)
  starting transfers between devices  9.45 us (6%)
  other arithmetic  2.75 us (2%)
    all_gather x2, waiting for transfers between devices, gathered(): far = lax.all_gather(near, ('z', 'core'), axis=0, tiled=True)  38.3 us
    all_gather x2, blocking collectives, gathered(): lax.all_gather(part.reshape(steps * PIECES, width), 'y', axis=0, tiled=True)  29.3 us
    all_to_all x1, waiting for transfers between devices, body(): lax.all_to_all(encoded, REPLICA, split_axis=0, concat_axis=0, tiled=True)  23.5 us
    pallas_call x2, Pallas kernels, run_window(): pl.pallas_call(functools.partial(window_kernel, steps, early), out_shape=...  19.7 us
    all_to_all x1, waiting for transfers between devices, body(): lax.all_to_all(jnp.broadcast_to(outer_shard, (groups, features, width)),...  10.9 us
    reshape x1, local copies, waits for them, and re-layouts, gathered(): return far.reshape(outer_ring * lanes * steps, columns)  8.27 us
    pallas_call x1, Pallas kernels, mix(): pl.pallas_call(mix_kernel, grid=(PIECES,), out_shape=jax.ShapeDtypeStruct...  6.28 us
    all_to_all x1, starting transfers between devices, body(): lax.all_to_all(encoded, REPLICA, split_axis=0, concat_axis=0, tiled=True)  4.92 us
  transfers between devices with their start and end apart: 4, of which 4 were waited for; matrix products, arithmetic and copies ran while one was open for 9% of the time, Pallas kernels for 12%

profile of v1, /device:TPU:1, one launch (start us, length us, event | category | flops | bytes accessed | tf_op | source)
XLA Modules:
  0.0 168.6 jit_solution(9010607044927872734)
XLA Ops:
  7.2 0.0 all-gather.5.cloned.1.call-start
  7.2 1.0 slice.15
  8.2 0.1 reshape.31
  8.3 16.5 %all_gather.14 = bf16[96,1792]{1,0:T(8,128)(2,1)} all-gather(bf16[24,1792]{1,0:T(8,128)(2,1)S(1)} %reshape.31), channel_id=1, replica_groups=mesh['z'=8,'y'=4,'core'=2,'y_lo'=2,'x'=4] {'y'}, dimensions={0}, use_global_device_ids=true | all-gather | bytes 430080 | tf_op jit(solution)/shard_map/all_gather | solution.py:174
  24.8 0.0 all-gather.3.cloned.1.call-start
  24.8 1.0 slice.14
  25.8 0.1 reshape.29
  25.9 12.9 %all_gather.12 = bf16[128,1792]{1,0:T(8,128)(2,1)S(1)} all-gather(bf16[32,1792]{1,0:T(8,128)(2,1)S(1)} %reshape.29), channel_id=1, replica_groups=mesh['z'=8,'y'=4,'core'=2,'y_lo'=2,'x'=4] {'y'}, dimensions={0}, use_global_device_ids=true | all-gather | bytes 573440 | tf_op jit(solution)/shard_map/all_gather | solution.py:174
  38.8 1.0 reshape.30
  39.9 38.0 %all-gather.5.cloned.1.call-done = bf16[1536,1792]{1,0:T(8,128)(2,1)} async-done(((bf16[96,1792]{1,0:T(8,128)(2,1)}), bf16[1536,1792]{1,0:T(8,128)(2,1)}) %all-gather.5.cloned.1.call-update) | async-done | bytes 5505040 | tf_op jit(solution)/shard_map/all_gather | solution.py:177
  77.9 8.3 %reshape.32.refs_0_ = bf16[192,14336]{1,0:T(8,128)(2,1)} reshape(bf16[1536,1792]{1,0:T(8,128)(2,1)} %all-gather.5.cloned.1.call-done) | data formatting | bytes 11010048 | tf_op jit(solution)/shard_map/reshape | solution.py:178
  86.2 8.9 %early_window.1.refs_2_ = bf16[8,64,1792]{2,1,0:T(8,128)(2,1)} custom-call(bf16[192,14336]{1,0:T(8,128)(2,1)} %reshape.32.refs_0_, bf16[64,14336]{1,0:T(8,128)(2,1)S(1)} %copy-done, bf16[192,64]{1,0:T(8,128)(2,1)S(1)} %reshape.33.refs_2_), custom_call_target="tpu_custom_call" | custom-call | flops 1761607680 | bytes 11010048 | tf_op jit(solution)/shard_map/early_window/pallas_call | solution.py:126
  95.1 4.9 %all-to-all-start = ((bf16[8,64,1792]{2,1,0:T(8,128)(2,1)}), bf16[8,64,1792]{2,1,0:T(8,128)(2,1)}, u32[]{:S(2)}, u32[]{:S(2)}) async-start(bf16[8,64,1792]{2,1,0:T(8,128)(2,1)} %early_window.1.refs_2_), calls=%async_computation | async-start | bytes 3670016 | tf_op jit(solution)/shard_map/all_to_all | solution.py:190
  100.0 23.5 %all-to-all-done = bf16[8,64,1792]{2,1,0:T(8,128)(2,1)} async-done(((bf16[8,64,1792]{2,1,0:T(8,128)(2,1)}), bf16[8,64,1792]{2,1,0:T(8,128)(2,1)}, u32[]{:S(2)}, u32[]{:S(2)}) %all-to-all-start) | async-done | bytes 1835040 | tf_op jit(solution)/shard_map/all_to_all | solution.py:190
  123.5 1.8 %convert_reduce_fusion = f32[64,1792]{1,0:T(8,128)S(1)} fusion(bf16[8,64,1792]{2,1,0:T(8,128)(2,1)} %all-to-all-done), kind=kLoop, calls=%fused_computation | loop fusion | flops 1720320 | bytes 2293760 | tf_op jit(solution)/shard_map/reduce_sum | solution.py:191
  125.4 0.9 subtract_convert_fusion
  126.3 1.3 broadcast_in_dim.6
  127.7 4.5 %all-to-all-start.1 = ((bf16[8,64,1792]{2,1,0:T(8,128)(2,1)}), bf16[8,64,1792]{2,1,0:T(8,128)(2,1)}, u32[]{:S(2)}, u32[]{:S(2)}) async-start(bf16[8,64,1792]{2,1,0:T(8,128)(2,1)} %broadcast_in_dim.6), calls=%async_computation.1 | async-start | bytes 3670016 | tf_op jit(solution)/shard_map/all_to_all | solution.py:199
  132.1 0.1 copy.10
  132.2 0.3 all-gather.3.cloned.1.call-done.refs_0_
  132.5 10.7 %late_window.1.late = bf16[64,14336]{1,0:T(8,128)(2,1)S(1)} custom-call(bf16[256,14336]{1,0:T(8,128)(2,1)} %all-gather.3.cloned.1.call-done.refs_0_, bf16[64,14336]{1,0:T(8,128)(2,1)S(1)} %copy-done, bf16[8,64,1792]{2,1,0:T(8,128)(2,1)} %early_window.1.refs_2_, bf16[256,64]{1,0:T(8,128)(2,1)S(1)} %bitcast.13), custom_call_target="tpu_custom_call" | custom-call | flops 2818572288 | bytes 14680064 | tf_op jit(solution)/shard_map/late_window/pallas_call | solution.py:126
  143.3 1.3 copy-done.1
  144.6 10.9 %all-to-all-done.1.outer = bf16[8,64,1792]{2,1,0:T(8,128)(2,1)} async-done(((bf16[8,64,1792]{2,1,0:T(8,128)(2,1)}), bf16[8,64,1792]{2,1,0:T(8,128)(2,1)}, u32[]{:S(2)}, u32[]{:S(2)}) %all-to-all-start.1) | async-done | bytes 1835040 | tf_op jit(solution)/shard_map/all_to_all | solution.py:199
  155.5 6.3 %mix.1 = bf16[64,14336]{1,0:T(8,128)(2,1)} custom-call(bf16[64,14336]{1,0:T(8,128)(2,1)} %copy-done.1, bf16[8,64,1792]{2,1,0:T(8,128)(2,1)} %all-to-all-done.1.outer), custom_call_target="tpu_custom_call" | custom-call | flops 2752512 | bytes 5505024 | tf_op jit(solution)/shard_map/mix/pallas_call | solution.py:152
  (15 shorter events, 0.1 us)
Async XLA Ops:
  7.2 32.6 %slice-start = ((bf16[1,7,64,64]{3,2,1,0:T(8,128)(2,1)}), bf16[1,3,64,64]{3,2,1,0:T(8,128)(2,1)S(1)}, s32[]{:S(2)}) async-start(bf16[1,7,64,64]{3,2,1,0:T(8,128)(2,1)} %param.7), calls=%async_computation.4 | async-start | bytes 98304 | tf_op jit(solution)/shard_map/slice | solution.py:186
  7.2 70.7 %all-gather.5.cloned.1.call-start = ((), (), s32[]{:S(2)}) async-start(), calls=%async_computation.3 | async-start | bytes 5849088 | tf_op jit(solution)/shard_map/all_gather | solution.py:177
  24.8 107.7 %all-gather.3.cloned.1.call-start = ((), (), s32[]{:S(2)}) async-start(), calls=%async_computation.2 | async-start | bytes 7798784 | tf_op jit(solution)/shard_map/all_gather | solution.py:177
  39.9 46.3 %copy-start = (bf16[64,14336]{1,0:T(8,128)(2,1)S(1)}, bf16[64,14336]{1,0:T(8,128)(2,1)}, u32[]{:S(2)}) copy-start(bf16[64,14336]{1,0:T(8,128)(2,1)} %refs_1_.3) | copy-start | bytes 5505028
  95.1 28.4 %all-to-all-start = ((bf16[8,64,1792]{2,1,0:T(8,128)(2,1)}), bf16[8,64,1792]{2,1,0:T(8,128)(2,1)}, u32[]{:S(2)}, u32[]{:S(2)}) async-start(bf16[8,64,1792]{2,1,0:T(8,128)(2,1)} %early_window.1.refs_2_), calls=%async_computation | async-start | bytes 3670016 | tf_op jit(solution)/shard_map/all_to_all | solution.py:190
  100.0 25.4 %copy-start.3 = (f32[64,1792]{1,0:T(8,128)S(1)}, f32[64,1792]{1,0:T(8,128)}, u32[]{:S(2)}) copy-start(f32[64,1792]{1,0:T(8,128)} %param.5) | copy-start | bytes 1376260
  126.3 1.4 copy-start.2
  127.6 4.5 %slice-start.1 = ((bf16[1,7,64,64]{3,2,1,0:T(8,128)(2,1)}), bf16[1,4,64,64]{3,2,1,0:T(8,128)(2,1)S(1)}, s32[]{:S(2)}) async-start(bf16[1,7,64,64]{3,2,1,0:T(8,128)(2,1)} %param.7), calls=%async_computation.5 | async-start | bytes 131072 | tf_op jit(solution)/shard_map/slice | solution.py:187
  127.7 27.8 %all-to-all-start.1 = ((bf16[8,64,1792]{2,1,0:T(8,128)(2,1)}), bf16[8,64,1792]{2,1,0:T(8,128)(2,1)}, u32[]{:S(2)}, u32[]{:S(2)}) async-start(bf16[8,64,1792]{2,1,0:T(8,128)(2,1)} %broadcast_in_dim.6), calls=%async_computation.1 | async-start | bytes 3670016 | tf_op jit(solution)/shard_map/all_to_all | solution.py:199
  143.3 1.3 copy-start.1
Sparse Core Ops, SparseCore 0:
  24.9 52.9 all-gather.4
  80.0 52.4 all-gather.2

commit v2 on v0

v2 whole, which is shorter than its diff:
```python
import functools
import math

import jax
import jax.numpy as jnp
from jax import lax
from jax.experimental import pallas as pl
from jax.experimental.pallas import tpu as pltpu
from jax.sharding import Mesh
from jax.sharding import PartitionSpec as P

BEFORE = 3
DURING = 4

inner_rate = 0.4
outer_rate = 0.7
momentum_rate = 0.9
mixing = 0.5

MESH_AXES = ("z", "y", "core", "y_lo", "x")
FSDP = ("z", "y", "core")
REPLICA = ("y_lo", "x")
RING = ("z", "core")
PIECES = 8
VMEM_LIMIT = 48 * 1024 * 1024
ACROSS = (((1,), (1,)), ((), ()))

def split_dot(high, low, short):
    product = jnp.dot(high, short, preferred_element_type=jnp.float32)
    return product + jnp.dot(low, short, preferred_element_type=jnp.float32)

def early_kernel(steps, hidden, weights, targets, out, hs, ws, outs, gram_ref, proj_ref, hidden_sem, weights_sem, out_sem):
    rows = hidden.shape[0]
    width = hs.shape[2]
    count = hs.shape[0]
    features = weights.shape[0]
    inverse_root = 1.0 / math.sqrt(weights.shape[1])
    def hidden_copy(piece):
        return pltpu.make_async_copy(hidden.at[:, pl.ds(piece * width, width)], hs.at[piece], hidden_sem.at[piece])
    def weights_copy(piece, side):
        return pltpu.make_async_copy(weights.at[:, pl.ds((side * count + piece) * width, width)],
            ws.at[piece, pl.ds(side * features, features)], weights_sem.at[side, piece])
    def out_copy(piece):
        return pltpu.make_async_copy(outs.at[piece], out.at[piece], out_sem.at[piece])
    for piece in range(count):
        hidden_copy(piece).start()
        weights_copy(piece, 0).start()
        weights_copy(piece, 1).start()
    proj_ref[...] = jnp.zeros_like(proj_ref)
    gram_ref[...] = jnp.zeros_like(gram_ref)
    def products(piece, carry):
        weights_copy(piece, 0).wait()
        weights_copy(piece, 1).wait()
        hidden_copy(piece).wait()
        block = hs[piece]
        proj_ref[...] += lax.dot_general(block, ws[piece], ACROSS, preferred_element_type=jnp.float32)
        gram_ref[...] += lax.dot_general(block, block, ACROSS, preferred_element_type=jnp.float32)
        return carry
    lax.fori_loop(0, count, products, 0)
    row = lax.broadcasted_iota(jnp.int32, (rows, features), 0)
    left = row % 2 == 0
    step_of = (row // 2) % steps
    def both(x):
        return x + jnp.where(left, pltpu.roll(x, rows - 1, 0), pltpu.roll(x, 1, 0))
    scaled = both(jnp.where(left, proj_ref[:, :features], proj_ref[:, features:])) * inverse_root
    gram = gram_ref[...]
    same = (lax.broadcasted_iota(jnp.int32, (rows, rows), 0) + lax.broadcasted_iota(jnp.int32, (rows, rows), 1)) % 2 == 0
    gram = jnp.where(same, gram, 0.0)
    high = gram.astype(jnp.bfloat16)
    low = (gram - high.astype(jnp.float32)).astype(jnp.bfloat16)
    wanted = targets[...].astype(jnp.float32)
    residual = jnp.zeros((rows, features), jnp.float32)
    for number in range(steps):
        moved = scaled
        if number:
            moved = scaled - (inner_rate * inverse_root * inverse_root) * both(split_dot(high, low, residual.astype(jnp.bfloat16)))
        fresh = (moved - wanted).astype(jnp.bfloat16).astype(jnp.float32)
        residual = jnp.where(step_of == number, fresh, residual)
    turned = jnp.concatenate([jnp.where(left, residual, 0.0), jnp.where(left, 0.0, residual)], axis=1).T.astype(jnp.bfloat16)
    def write(piece, carry):
        update = (inner_rate * inverse_root) * jnp.dot(turned, hs[piece], preferred_element_type=jnp.float32)
        encoded = update.astype(jnp.bfloat16)
        outs[piece] = encoded[:features]
        outs[count + piece] = encoded[features:]
        out_copy(piece).start()
        out_copy(count + piece).start()
        return carry
    lax.fori_loop(0, count, write, 0)
    for piece in range(PIECES):
        out_copy(piece).wait()

def early_window(steps, hidden, weights, targets):
    rows = hidden.shape[0]
    features, columns = weights.shape
    width = columns // PIECES
    count = PIECES // 2
    anywhere = pl.BlockSpec(memory_space=pltpu.HBM)
    return pl.pallas_call(
        functools.partial(early_kernel, steps),
        out_shape=pltpu.HBM((PIECES, features, width), jnp.bfloat16),
        in_specs=[anywhere, anywhere, pl.BlockSpec(memory_space=pltpu.VMEM)],
        out_specs=anywhere,
        scratch_shapes=[
            pltpu.VMEM((count, rows, width), jnp.bfloat16),
            pltpu.VMEM((count, 2 * features, width), jnp.bfloat16),
            pltpu.VMEM((PIECES, features, width), jnp.bfloat16),
            pltpu.VMEM((rows, rows), jnp.float32),
            pltpu.VMEM((rows, 2 * features), jnp.float32),
            pltpu.SemaphoreType.DMA((count,)),
            pltpu.SemaphoreType.DMA((2, count)),
            pltpu.SemaphoreType.DMA((PIECES,)),
        ],
        compiler_params=pltpu.CompilerParams(vmem_limit_bytes=VMEM_LIMIT),
        cost_estimate=pl.CostEstimate(flops=2*rows*columns*rows, bytes_accessed=rows*columns+4*features*columns, transcendentals=0),
        name="early_window")(hidden, weights, targets)

def late_kernel(steps, hidden, weights, encoded, targets, out, hs, ws, es, outs, gram_ref, proj_ref, hidden_sem, weights_sem, enc_sem, out_sem):
    rows = hidden.shape[0]
    width = hs.shape[2]
    features = weights.shape[0]
    inverse_root = 1.0 / math.sqrt(weights.shape[1])
    def hidden_copy(piece):
        return pltpu.make_async_copy(hidden.at[:, pl.ds(piece * width, width)], hs.at[piece], hidden_sem.at[piece])
    def weights_copy(piece):
        return pltpu.make_async_copy(weights.at[:, pl.ds(piece * width, width)], ws.at[piece], weights_sem.at[piece])
    def enc_copy(piece):
        return pltpu.make_async_copy(encoded.at[piece], es.at[piece], enc_sem.at[piece])
    def out_copy(piece):
        return pltpu.make_async_copy(outs.at[piece], out.at[:, pl.ds(piece * width, width)], out_sem.at[piece])
    for piece in range(PIECES):
        weights_copy(piece).start()
        enc_copy(piece).start()
        hidden_copy(piece).start()
    proj_ref[...] = jnp.zeros_like(proj_ref)
    gram_ref[...] = jnp.zeros_like(gram_ref)
    def products(piece, carry):
        weights_copy(piece).wait()
        enc_copy(piece).wait()
        current = (ws[piece].astype(jnp.float32) - es[piece].astype(jnp.float32)).astype(jnp.bfloat16)
        ws[piece] = current
        hidden_copy(piece).wait()
        block = hs[piece]
        proj_ref[...] += lax.dot_general(block, current, ACROSS, preferred_element_type=jnp.float32)
        gram_ref[...] += lax.dot_general(block, block, ACROSS, preferred_element_type=jnp.float32)
        return carry
    lax.fori_loop(0, PIECES, products, 0)
    step_of = lax.broadcasted_iota(jnp.int32, (rows, features), 0) % steps
    scaled = proj_ref[...] * inverse_root
    gram = gram_ref[...]
    high = gram.astype(jnp.bfloat16)
    low = (gram - high.astype(jnp.float32)).astype(jnp.bfloat16)
    wanted = targets[...].astype(jnp.float32)
    residual = jnp.zeros((rows, features), jnp.float32)
    for number in range(steps):
        moved = scaled
        if number:
            moved = scaled - (inner_rate * inverse_root * inverse_root) * split_dot(high, low, residual.astype(jnp.bfloat16))
        fresh = (moved - wanted).astype(jnp.bfloat16).astype(jnp.float32)
        residual = jnp.where(step_of == number, fresh, residual)
    turned = residual.T.astype(jnp.bfloat16)
    def write(piece, carry):
        update = (inner_rate * inverse_root) * jnp.dot(turned, hs[piece], preferred_element_type=jnp.float32)
        outs[piece] = (ws[piece].astype(jnp.float32) - update).astype(jnp.bfloat16)
        out_copy(piece).start()
        return carry
    lax.fori_loop(0, PIECES, write, 0)
    for piece in range(PIECES):
        out_copy(piece).wait()

def late_window(steps, hidden, weights, encoded, targets):
    rows = hidden.shape[0]
    features, columns = weights.shape
    width = columns // PIECES
    anywhere = pl.BlockSpec(memory_space=pltpu.HBM)
    held = pltpu.VMEM((PIECES, features, width), jnp.bfloat16)
    sems = pltpu.SemaphoreType.DMA((PIECES,))
    return pl.pallas_call(
        functools.partial(late_kernel, steps),
        out_shape=pltpu.HBM((features, columns), jnp.bfloat16),
        in_specs=[anywhere]*3+[pl.BlockSpec(memory_space=pltpu.VMEM)],
        out_specs=anywhere,
        scratch_shapes=[pltpu.VMEM((PIECES, rows, width), jnp.bfloat16), held, held, held,
            pltpu.VMEM((rows, rows), jnp.float32), pltpu.VMEM((rows, features), jnp.float32),
            sems, sems, sems, sems],
        compiler_params=pltpu.CompilerParams(vmem_limit_bytes=VMEM_LIMIT),
        cost_estimate=pl.CostEstimate(flops=2*rows*columns*(rows+2*features), bytes_accessed=2*columns*(rows+4*features), transcendentals=0),
        name="late_window")(hidden, weights, encoded, targets)

def outer_kernel(offset, received, momentum, weights, shard, momentum_out, copies, rs, ms, ws, os_, in_sem, out_sem):
    groups = received.shape[0]
    half = received.shape[1]
    width = received.shape[2]
    begin = pl.multiple_of(offset[0] * width, 128)
    loads = [pltpu.make_async_copy(momentum, ms, in_sem.at[groups]),
             pltpu.make_async_copy(weights.at[:, pl.ds(begin, width)], ws, in_sem.at[groups + 1])]
    loads += [pltpu.make_async_copy(received.at[g], rs.at[g], in_sem.at[g]) for g in range(groups)]
    for load in loads: load.start()
    total = jnp.zeros((half, width), jnp.float32)
    for load in loads: load.wait()
    for g in range(groups):
        total += rs[g].astype(jnp.float32)
    average = total / groups
    fresh = momentum_rate * ms[...] + average
    ms[...] = fresh
    os_[...] = (ws[...].astype(jnp.float32) - outer_rate * (average + momentum_rate * fresh)).astype(jnp.bfloat16)
    stores = [pltpu.make_async_copy(os_, copies.at[g], out_sem.at[g]) for g in range(groups)]
    stores += [pltpu.make_async_copy(os_, shard, out_sem.at[groups]),
               pltpu.make_async_copy(ms, momentum_out, out_sem.at[groups + 1])]
    for store in stores: store.start()
    for store in stores: store.wait()

def outer_step(offset, received, momentum, weights):
    groups, half, width = received.shape
    anywhere = pl.BlockSpec(memory_space=pltpu.HBM)
    sems = pltpu.SemaphoreType.DMA((groups + 2,))
    return pl.pallas_call(
        outer_kernel,
        out_shape=(pltpu.HBM(momentum.shape, jnp.bfloat16), pltpu.HBM(momentum.shape, jnp.float32),
                   pltpu.HBM(received.shape, jnp.bfloat16)),
        in_specs=[pl.BlockSpec(memory_space=pltpu.SMEM)] + [anywhere]*3,
        out_specs=(anywhere,)*3,
        scratch_shapes=[pltpu.VMEM(received.shape, jnp.bfloat16), pltpu.VMEM((half, width), jnp.float32),
            pltpu.VMEM((half, width), jnp.bfloat16), pltpu.VMEM((half, width), jnp.bfloat16), sems, sems],
        compiler_params=pltpu.CompilerParams(vmem_limit_bytes=VMEM_LIMIT),
        cost_estimate=pl.CostEstimate(flops=groups*half*width, bytes_accessed=4*groups*half*width, transcendentals=0),
        name="outer_step")(offset, received, momentum, weights)

def mix_kernel(late, outer, out, ls, os_, ns, late_sem, outer_sem, out_sem):
    width = ls.shape[2]
    def late_copy(p): return pltpu.make_async_copy(late.at[:, pl.ds(p * width, width)], ls.at[p], late_sem.at[p])
    def outer_copy(p): return pltpu.make_async_copy(outer.at[p], os_.at[p], outer_sem.at[p])
    def out_copy(p): return pltpu.make_async_copy(ns.at[p], out.at[:, pl.ds(p * width, width)], out_sem.at[p])
    for p in range(PIECES):
        late_copy(p).start(); outer_copy(p).start()
    for p in range(PIECES):
        late_copy(p).wait(); outer_copy(p).wait()
        ns[p] = (mixing * ls[p].astype(jnp.float32) + (1.0 - mixing) * os_[p].astype(jnp.float32)).astype(jnp.bfloat16)
        out_copy(p).start()
    for p in range(PIECES):
        out_copy(p).wait()

def mix(late, outer):
    features, columns = late.shape
    width = columns // PIECES
    anywhere = pl.BlockSpec(memory_space=pltpu.HBM)
    held = pltpu.VMEM((PIECES, features, width), jnp.bfloat16)
    sems = pltpu.SemaphoreType.DMA((PIECES,))
    return pl.pallas_call(mix_kernel, out_shape=pltpu.HBM((features, columns), jnp.bfloat16),
        in_specs=[anywhere]*2, out_specs=anywhere,
        scratch_shapes=[held]*3+[sems]*3,
        compiler_params=pltpu.CompilerParams(vmem_limit_bytes=VMEM_LIMIT),
        cost_estimate=pl.CostEstimate(flops=3*features*columns, bytes_accessed=6*features*columns, transcendentals=0),
        name="mix")(late, outer)


def body(weights, momentum, hidden, targets):
    features, columns = weights.shape
    width = columns // PIECES
    lanes = lax.axis_size("y")
    depth = lax.axis_size("z")
    cores = lax.axis_size("core")
    own = hidden.reshape(BEFORE + DURING, PIECES, width)

    def near_rows(part, steps):
        return lax.all_gather(part.reshape(steps * PIECES, width), "y", axis=0, tiled=True)

    def target_rows(part, steps):
        parts = part.reshape(steps, depth, lanes, cores, features)
        return parts.transpose(1, 3, 2, 0, 4).reshape(-1, features)

    early_near = near_rows(own[:BEFORE], BEFORE).reshape(2 * lanes * BEFORE, columns // 2)
    early_hidden = lax.all_gather(early_near, RING, axis=0, tiled=True)
    late_near = near_rows(own[BEFORE:], DURING).reshape(lanes * DURING, columns)
    late_hidden = lax.all_gather(late_near, RING, axis=0, tiled=True)
    early_targets = jnp.repeat(target_rows(targets[0, :BEFORE], BEFORE), 2, axis=0)
    late_targets = target_rows(targets[0, BEFORE:], DURING)

    encoded = early_window(BEFORE, early_hidden, weights, early_targets)

    def swap(x):
        moved = lax.all_to_all(x, REPLICA, split_axis=0, concat_axis=0, tiled=True)
        return pltpu.with_memory_space_constraint(moved, pltpu.HBM)

    place = lax.axis_index(REPLICA).astype(jnp.int32)[None]
    outer_shard, momentum_out, copies = outer_step(place, swap(encoded), momentum, weights)
    outer = swap(copies)

    late = late_window(DURING, late_hidden, weights, encoded, late_targets)
    new_weights = mix(late, outer)[None]
    return (new_weights, outer_shard, momentum_out)


def solution(mesh):
    fine = Mesh(mesh.devices.reshape(8, 4, 2, 2, 4), MESH_AXES)
    placed = (
        P(FSDP, None),
        P(FSDP, REPLICA),
        P(REPLICA, None, FSDP, None),
        P(REPLICA, None, None, FSDP),
    )
    return jax.shard_map(
        body,
        mesh=fine,
        in_specs=placed,
        out_specs=(P(REPLICA, FSDP, None), P(FSDP, REPLICA), P(FSDP, REPLICA)),
        check_vma=False,
    )
```

time: 735 us -> 160 us (0.22)
  waiting for transfers between devices: 655 us -> 71.6 us
  matrix products: 54.2 us -> 0 us
  blocking collectives: 0 us -> 29 us
  Pallas kernels: 0 us -> 28.8 us
  starting transfers between devices: 0.53 us -> 9.58 us
    all_gather x8 -> x2, waiting for transfers between devices: 616 us -> 45.9 us  [the longest x1 38.5 us: body(): early_hidden = lax.all_gather(early_near, RING, axis=0, tiled=True)]
    dot_general x7 -> x0, matrix products: 54.2 us -> none  [advance(): lax.dot_general(residual, hidden_rows, (((0,), (0,)), ((), ())), preferre...]
    reduce_scatter x1 -> x0, waiting for transfers between devices: 35.8 us -> none  [synchronize(): lax.psum_scatter(encoded.astype(jnp.float32).astype(jnp.bfloat16), 'repli...]
    all_gather x0 -> x2, blocking collectives: none -> 29 us  [near_rows(): lax.all_gather(part.reshape(steps * PIECES, width), 'y', axis=0, tiled=True)]
    pallas_call x0 -> x4, Pallas kernels: none -> 28.8 us  [the longest x1 12.2 us: late_window(): pl.pallas_call(functools.partial(late_kernel, steps), out_shape=pltpu.HBM...]
    all_to_all x0 -> x2, waiting for transfers between devices: none -> 25.6 us  [swap(): moved = lax.all_to_all(x, REPLICA, split_axis=0, concat_axis=0, tiled=True)]
    all_to_all x0 -> x2, starting transfers between devices: none -> 9.5 us  [swap(): moved = lax.all_to_all(x, REPLICA, split_axis=0, concat_axis=0, tiled=True)]
  transfers between devices with their start and end apart: 9 -> 4, of which waited for: 9 -> 4; matrix products, arithmetic and copies ran while one was open for 6% -> 1% of each run, Pallas kernels for 0% -> 16%
where the time goes in v2:
time: 160 us
  waiting for transfers between devices  71.6 us (45%)
  blocking collectives  29 us (18%)
  Pallas kernels  28.8 us (18%)
  between operations  14.2 us (9%)
  starting transfers between devices  9.58 us (6%)
  local copies, waits for them, and re-layouts  6.47 us (4%)
    all_gather x1, waiting for transfers between devices, body(): early_hidden = lax.all_gather(early_near, RING, axis=0, tiled=True)  38.5 us
    all_gather x2, blocking collectives, near_rows(): lax.all_gather(part.reshape(steps * PIECES, width), 'y', axis=0, tiled=True)  29 us
    all_to_all x2, waiting for transfers between devices, swap(): moved = lax.all_to_all(x, REPLICA, split_axis=0, concat_axis=0, tiled=True)  25.6 us
    pallas_call x1, Pallas kernels, late_window(): pl.pallas_call(functools.partial(late_kernel, steps), out_shape=pltpu.HBM...  12.2 us
    pallas_call x1, Pallas kernels, early_window(): pl.pallas_call(functools.partial(early_kernel, steps), out_shape=pltpu.HB...  10 us
    all_to_all x2, starting transfers between devices, swap(): moved = lax.all_to_all(x, REPLICA, split_axis=0, concat_axis=0, tiled=True)  9.5 us
    all_gather x1, waiting for transfers between devices, body(): late_hidden = lax.all_gather(late_near, RING, axis=0, tiled=True)  7.47 us
    pallas_call x1, Pallas kernels, outer_step(): pl.pallas_call(outer_kernel, out_shape=(pltpu.HBM(momentum.shape, jnp.bfl...  3.89 us
  transfers between devices with their start and end apart: 4, of which 4 were waited for; matrix products, arithmetic and copies ran while one was open for 1% of the time, Pallas kernels for 16%

profile of v2, /device:TPU:1, one launch (start us, length us, event | category | flops | bytes accessed | tf_op | source)
XLA Modules:
  0.0 159.6 jit_solution(16481515514518850983)
XLA Ops:
  7.2 0.0 all-gather.5.cloned.1.call-start
  7.2 1.0 slice.15
  8.2 0.1 reshape.34
  8.4 16.0 %all_gather.14 = bf16[96,1792]{1,0:T(8,128)(2,1)S(1)} all-gather(bf16[24,1792]{1,0:T(8,128)(2,1)S(1)} %reshape.34), channel_id=1, replica_groups=mesh['z'=8,'y'=4,'core'=2,'y_lo'=2,'x'=4] {'y'}, dimensions={0}, use_global_device_ids=true | all-gather | bytes 430080 | tf_op jit(solution)/shard_map/all_gather | solution.py:265
  24.3 1.0 reshape.35
  25.3 0.0 all-gather.3.cloned.1.call-start
  25.4 0.1 slice.14
  25.4 0.1 reshape.32
  25.5 13.1 %all_gather.12 = bf16[128,1792]{1,0:T(8,128)(2,1)S(1)} all-gather(bf16[32,1792]{1,0:T(8,128)(2,1)S(1)} %reshape.32), channel_id=1, replica_groups=mesh['z'=8,'y'=4,'core'=2,'y_lo'=2,'x'=4] {'y'}, dimensions={0}, use_global_device_ids=true | all-gather | bytes 573440 | tf_op jit(solution)/shard_map/all_gather | solution.py:265
  38.6 1.0 reshape.33
  39.7 38.5 %all-gather.5.cloned.1.call-done.hidden = bf16[384,7168]{1,0:T(8,128)(2,1)} async-done(((bf16[24,7168]{1,0:T(8,128)(2,1)}), bf16[384,7168]{1,0:T(8,128)(2,1)}) %all-gather.5.cloned.1.call-update) | async-done | bytes 5505040 | tf_op jit(solution)/shard_map/all_gather | solution.py:272
  78.2 0.1 broadcast_in_dim.9
  78.3 10.0 %early_window.1.encoded = bf16[8,64,1792]{2,1,0:T(8,128)(2,1)} custom-call(bf16[384,7168]{1,0:T(8,128)(2,1)} %all-gather.5.cloned.1.call-done.hidden, bf16[64,14336]{1,0:T(8,128)(2,1)S(1)} %copy-done.1, bf16[384,64]{1,0:T(8,128)(2,1)S(1)} %bitcast.16), custom_call_target="tpu_custom_call" | custom-call | flops 4227858432 | bytes 9175040 | tf_op jit(solution)/shard_map/early_window/pallas_call | solution.py:98
  88.3 5.0 %all-to-all-start = ((bf16[8,64,1792]{2,1,0:T(8,128)(2,1)}), bf16[8,64,1792]{2,1,0:T(8,128)(2,1)}, u32[]{:S(2)}, u32[]{:S(2)}) async-start(bf16[8,64,1792]{2,1,0:T(8,128)(2,1)} %early_window.1.encoded), calls=%async_computation | async-start | bytes 3670016 | tf_op jit(solution)/shard_map/all_to_all | solution.py:281
  93.4 23.5 %all-to-all-done.received = bf16[8,64,1792]{2,1,0:T(8,128)(2,1)} async-done(((bf16[8,64,1792]{2,1,0:T(8,128)(2,1)}), bf16[8,64,1792]{2,1,0:T(8,128)(2,1)}, u32[]{:S(2)}, u32[]{:S(2)}) %all-to-all-start) | async-done | bytes 1835040 | tf_op jit(solution)/shard_map/all_to_all | solution.py:281
  116.9 3.9 %outer_step.1 = (bf16[64,1792]{1,0:T(8,128)(2,1)}, f32[64,1792]{1,0:T(8,128)}, bf16[8,64,1792]{2,1,0:T(8,128)(2,1)}) custom-call(s32[1]{0:T(128)} %bitcast.6.offset, bf16[8,64,1792]{2,1,0:T(8,128)(2,1)} %all-to-all-done.received, f32[64,1792]{1,0:T(8,128)S(1)} %copy-done.4, bf16[64,14336]{1,0:T(8,128)(2,1)S(1)} %copy-done.1), custom_call_target="tpu_custom_call" | custom-call | flops 917504 | bytes 3670016 | tf_op jit(solution)/shard_map/outer_step/pallas_call | solution.py:216
  120.8 4.5 %all-to-all-start.1 = ((bf16[8,64,1792]{2,1,0:T(8,128)(2,1)}), bf16[8,64,1792]{2,1,0:T(8,128)(2,1)}, u32[]{:S(2)}, u32[]{:S(2)}) async-start(bf16[8,64,1792]{2,1,0:T(8,128)(2,1)} %get-tuple-element.6), calls=%async_computation.1 | async-start | bytes 3670016 | tf_op jit(solution)/shard_map/all_to_all | solution.py:281
  125.3 0.1 copy.9
  125.3 7.5 %all-gather.3.cloned.1.call-done.hidden = bf16[256,14336]{1,0:T(8,128)(2,1)} async-done(((bf16[16,14336]{1,0:T(8,128)(2,1)}), bf16[256,14336]{1,0:T(8,128)(2,1)}) %all-gather.3.cloned.1.call-update) | async-done | bytes 7340048 | tf_op jit(solution)/shard_map/all_gather | solution.py:274
  132.8 1.5 copy-done.2
  134.3 12.2 %late_window.1.late = bf16[64,14336]{1,0:T(8,128)(2,1)} custom-call(bf16[256,14336]{1,0:T(8,128)(2,1)} %all-gather.3.cloned.1.call-done.hidden, bf16[64,14336]{1,0:T(8,128)(2,1)S(1)} %copy-done.2, bf16[8,64,1792]{2,1,0:T(8,128)(2,1)S(1)} %copy-done, bf16[256,64]{1,0:T(8,128)(2,1)S(1)} %bitcast.15), custom_call_target="tpu_custom_call" | custom-call | flops 2818572288 | bytes 14680064 | tf_op jit(solution)/shard_map/late_window/pallas_call | solution.py:177
  146.5 2.1 %all-to-all-done.1.outer = bf16[8,64,1792]{2,1,0:T(8,128)(2,1)} async-done(((bf16[8,64,1792]{2,1,0:T(8,128)(2,1)}), bf16[8,64,1792]{2,1,0:T(8,128)(2,1)}, u32[]{:S(2)}, u32[]{:S(2)}) %all-to-all-start.1) | async-done | bytes 1835040 | tf_op jit(solution)/shard_map/all_to_all | solution.py:281
  148.6 1.5 copy-done.3
  150.1 2.7 %mix.1 = bf16[64,14336]{1,0:T(8,128)(2,1)} custom-call(bf16[64,14336]{1,0:T(8,128)(2,1)S(1)} %copy-done.3, bf16[8,64,1792]{2,1,0:T(8,128)(2,1)} %all-to-all-done.1.outer), custom_call_target="tpu_custom_call" | custom-call | flops 2752512 | bytes 5505024 | tf_op jit(solution)/shard_map/mix/pallas_call | solution.py:248
  (18 shorter events, 0.2 us)
Async XLA Ops:
  7.2 18.2 %copy-start.5 = (bf16[1,7,1,14336]{3,1,2,0:T(8,128)(2,1)S(1)}, bf16[1,7,1,14336]{3,1,2,0:T(8,128)(2,1)}, u32[]{:S(2)}) copy-start(bf16[1,7,1,14336]{3,1,2,0:T(8,128)(2,1)} %param.6) | copy-start | bytes 602116
  7.2 71.0 %all-gather.5.cloned.1.call-start = ((), (), s32[]{:S(2)}) async-start(), calls=%async_computation.3 | async-start | bytes 5849088 | tf_op jit(solution)/shard_map/all_gather | solution.py:272
  24.3 15.3 %slice-start = ((bf16[1,7,64,64]{3,2,1,0:T(8,128)(2,1)}), bf16[1,3,64,64]{3,2,1,0:T(8,128)(2,1)S(1)}, s32[]{:S(2)}) async-start(bf16[1,7,64,64]{3,2,1,0:T(8,128)(2,1)} %param.7), calls=%async_computation.4 | async-start | bytes 98304 | tf_op jit(solution)/shard_map/slice | solution.py:275
  24.3 53.9 %copy-start.1 = (bf16[64,14336]{1,0:T(8,128)(2,1)S(1)}, bf16[64,14336]{1,0:T(8,128)(2,1)}, u32[]{:S(2)}) copy-start(bf16[64,14336]{1,0:T(8,128)(2,1)} %weights.5) | copy-start | bytes 5505028
  25.3 107.5 %all-gather.3.cloned.1.call-start = ((), (), s32[]{:S(2)}) async-start(), calls=%async_computation.2 | async-start | bytes 7798784 | tf_op jit(solution)/shard_map/all_gather | solution.py:274
  88.3 28.6 %copy-start.4 = (f32[64,1792]{1,0:T(8,128)S(1)}, f32[64,1792]{1,0:T(8,128)}, u32[]{:S(2)}) copy-start(f32[64,1792]{1,0:T(8,128)} %momentum.1) | copy-start | bytes 1376260
  88.3 28.5 %all-to-all-start = ((bf16[8,64,1792]{2,1,0:T(8,128)(2,1)}), bf16[8,64,1792]{2,1,0:T(8,128)(2,1)}, u32[]{:S(2)}, u32[]{:S(2)}) async-start(bf16[8,64,1792]{2,1,0:T(8,128)(2,1)} %early_window.1.encoded), calls=%async_computation | async-start | bytes 3670016 | tf_op jit(solution)/shard_map/all_to_all | solution.py:281
  120.8 4.5 %slice-start.1 = ((bf16[1,7,64,64]{3,2,1,0:T(8,128)(2,1)}), bf16[1,4,64,64]{3,2,1,0:T(8,128)(2,1)S(1)}, s32[]{:S(2)}) async-start(bf16[1,7,64,64]{3,2,1,0:T(8,128)(2,1)} %param.7), calls=%async_computation.5 | async-start | bytes 131072 | tf_op jit(solution)/shard_map/slice | solution.py:276
  120.8 12.0 %copy-start = (bf16[8,64,1792]{2,1,0:T(8,128)(2,1)S(1)}, bf16[8,64,1792]{2,1,0:T(8,128)(2,1)}, u32[]{:S(2)}) copy-start(bf16[8,64,1792]{2,1,0:T(8,128)(2,1)} %early_window.1.encoded) | copy-start | bytes 5505028
  120.8 27.8 %all-to-all-start.1 = ((bf16[8,64,1792]{2,1,0:T(8,128)(2,1)}), bf16[8,64,1792]{2,1,0:T(8,128)(2,1)}, u32[]{:S(2)}, u32[]{:S(2)}) async-start(bf16[8,64,1792]{2,1,0:T(8,128)(2,1)} %get-tuple-element.6), calls=%async_computation.1 | async-start | bytes 3670016 | tf_op jit(solution)/shard_map/all_to_all | solution.py:281
  132.8 1.5 copy-start.2
  148.6 1.5 copy-start.3
Sparse Core Ops, SparseCore 0:
  25.4 52.7 all-gather.4
  80.3 52.4 all-gather.2

commit v3 on v0

v3 whole, which is shorter than its diff:
```python
import functools
import math

import jax
import jax.numpy as jnp
from jax import lax
from jax.experimental import pallas as pl
from jax.experimental.pallas import tpu as pltpu
from jax.sharding import Mesh
from jax.sharding import PartitionSpec as P

BEFORE = 3
DURING = 4

inner_rate = 0.4
outer_rate = 0.7
momentum_rate = 0.9
mixing = 0.5

MESH_AXES = ("z", "y", "core", "y_lo", "x")
FSDP = ("z", "y", "core")
REPLICA = ("y_lo", "x")
RING = ("z", "core")
PIECES = 8
VMEM_LIMIT = 48 * 1024 * 1024
AHEAD = 3
ACROSS = (((1,), (1,)), ((), ()))


def in_order(count, start, use, unroll):
    for piece in range(min(AHEAD, count)):
        start(piece)

    def turn(piece, carry):
        @pl.when(piece + AHEAD < count)
        def _():
            start(piece + AHEAD)

        use(piece)
        return carry

    lax.fori_loop(0, count, turn, 0, unroll=unroll)


def solve(steps, step_of, scaled, gram, wanted, moved_by, total):
    high = gram.astype(jnp.bfloat16)
    low = (gram - high.astype(jnp.float32)).astype(jnp.bfloat16)
    residual = jnp.zeros_like(scaled)
    for number in range(steps):
        moved = scaled
        if number:
            short = residual.astype(jnp.bfloat16)
            product = jnp.dot(short, high, preferred_element_type=jnp.float32)
            product += jnp.dot(short, low, preferred_element_type=jnp.float32)
            moved = scaled - moved_by * total(product)
        fresh = (moved - wanted).astype(jnp.bfloat16).astype(jnp.float32)
        residual = jnp.where(step_of == number, fresh, residual)
    return residual


def early_kernel(steps, hidden, weights, targets, out, held, outs, both_ref, hidden_sem,
                 weights_sem, out_sem):
    rows = hidden.shape[0]
    count, _, width = held.shape
    features = weights.shape[0]
    top = 2 * features
    inverse_root = 1.0 / math.sqrt(weights.shape[1])

    def copies(piece):
        yield pltpu.make_async_copy(
            hidden.at[:, pl.ds(piece * width, width)], held.at[piece, pl.ds(top, rows)],
            hidden_sem.at[piece])
        for side in range(2):
            yield pltpu.make_async_copy(
                weights.at[:, pl.ds((side * count + piece) * width, width)],
                held.at[piece, pl.ds(side * features, features)], weights_sem.at[side, piece])

    def out_copy(piece):
        return pltpu.make_async_copy(outs.at[piece], out.at[piece], out_sem.at[piece])

    def start(piece):
        for copy in copies(piece):
            copy.start()

    def products(piece):
        for copy in copies(piece):
            copy.wait()
        both_ref[...] += lax.dot_general(
            held[piece, top:], held[piece], ACROSS, preferred_element_type=jnp.float32)

    both_ref[...] = jnp.zeros_like(both_ref)
    in_order(count, start, products, count)

    column = lax.broadcasted_iota(jnp.int32, (features, rows), 1)
    left = column % 2 == 0

    def total(x):
        return x + jnp.where(left, pltpu.roll(x, rows - 1, 1), pltpu.roll(x, 1, 1))

    projected = both_ref[:, :top].T
    scaled = total(jnp.where(left, projected[:features], projected[features:])) * inverse_root
    apart = (lax.broadcasted_iota(jnp.int32, (rows, rows), 0)
             + lax.broadcasted_iota(jnp.int32, (rows, rows), 1)) % 2
    gram = jnp.where(apart == 0, both_ref[:, top:], 0.0)
    residual = solve(steps, (column // 2) % steps, scaled, gram, targets[...].astype(jnp.float32),
                     inner_rate * inverse_root * inverse_root, total)
    factors = jnp.concatenate(
        [jnp.where(left, residual, 0.0), jnp.where(left, 0.0, residual)], axis=0
    ).astype(jnp.bfloat16)

    def write(piece, carry):
        update = (inner_rate * inverse_root) * jnp.dot(
            factors, held[piece, top:], preferred_element_type=jnp.float32)
        encoded = update.astype(jnp.bfloat16)
        outs[piece] = encoded[:features]
        outs[count + piece] = encoded[features:]
        out_copy(piece).start()
        out_copy(count + piece).start()
        return carry

    lax.fori_loop(0, count, write, 0, unroll=4)
    for piece in range(PIECES):
        out_copy(piece).wait()


def early_window(steps, hidden, weights, targets):
    rows = hidden.shape[0]
    features, columns = weights.shape
    width = columns // PIECES
    count = PIECES // 2
    anywhere = pl.BlockSpec(memory_space=pl.ANY)
    return pl.pallas_call(
        functools.partial(early_kernel, steps),
        out_shape=pltpu.HBM((PIECES, features, width), jnp.bfloat16),
        in_specs=[anywhere, anywhere, pl.BlockSpec(memory_space=pltpu.VMEM)],
        out_specs=anywhere,
        scratch_shapes=[
            pltpu.VMEM((count, 2 * features + rows, width), jnp.bfloat16),
            pltpu.VMEM((PIECES, features, width), jnp.bfloat16),
            pltpu.VMEM((rows, 2 * features + rows), jnp.float32),
            pltpu.SemaphoreType.DMA((count,)),
            pltpu.SemaphoreType.DMA((2, count)),
            pltpu.SemaphoreType.DMA((PIECES,)),
        ],
        compiler_params=pltpu.CompilerParams(vmem_limit_bytes=VMEM_LIMIT),
        cost_estimate=pl.CostEstimate(
            flops=rows * columns * (rows + 4 * features),
            bytes_accessed=columns * (rows + 4 * features), transcendentals=0),
        name="early_window",
    )(hidden, weights, targets)


def late_kernel(steps, hidden, base, targets, out, held, outs, both_ref, hidden_sem, base_sem,
                out_sem):
    rows = hidden.shape[0]
    count, features, width = base.shape
    inverse_root = 1.0 / math.sqrt(hidden.shape[1])

    def copies(piece):
        yield pltpu.make_async_copy(
            hidden.at[:, pl.ds(piece * width, width)], held.at[piece, pl.ds(features, rows)],
            hidden_sem.at[piece])
        yield pltpu.make_async_copy(
            base.at[piece], held.at[piece, pl.ds(0, features)], base_sem.at[piece])

    def out_copy(piece):
        return pltpu.make_async_copy(
            outs.at[piece], out.at[:, pl.ds(piece * width, width)], out_sem.at[piece])

    def start(piece):
        for copy in copies(piece):
            copy.start()

    def products(piece):
        for copy in copies(piece):
            copy.wait()
        both_ref[...] += lax.dot_general(
            held[piece], held[piece, features:], ACROSS, preferred_element_type=jnp.float32)

    both_ref[...] = jnp.zeros_like(both_ref)
    in_order(count, start, products, 1)

    step_of = lax.broadcasted_iota(jnp.int32, (features, rows), 1) % steps
    residual = solve(steps, step_of, both_ref[:features] * inverse_root, both_ref[features:],
                     targets[...].astype(jnp.float32), inner_rate * inverse_root * inverse_root,
                     lambda x: x)
    factors = residual.astype(jnp.bfloat16)

    def write(piece, carry):
        update = (inner_rate * inverse_root) * jnp.dot(
            factors, held[piece, features:], preferred_element_type=jnp.float32)
        outs[piece] = (held[piece, :features].astype(jnp.float32) - update).astype(jnp.bfloat16)
        out_copy(piece).start()
        return carry

    lax.fori_loop(0, count, write, 0, unroll=4)
    for piece in range(count):
        out_copy(piece).wait()


def late_window(steps, hidden, base, targets):
    rows, columns = hidden.shape
    count, features, width = base.shape
    anywhere = pl.BlockSpec(memory_space=pl.ANY)
    semaphores = pltpu.SemaphoreType.DMA((count,))
    return pl.pallas_call(
        functools.partial(late_kernel, steps),
        out_shape=pltpu.HBM((features, columns), jnp.bfloat16),
        in_specs=[anywhere, anywhere, pl.BlockSpec(memory_space=pltpu.VMEM)],
        out_specs=anywhere,
        scratch_shapes=[
            pltpu.VMEM((count, features + rows, width), jnp.bfloat16),
            pltpu.VMEM((count, features, width), jnp.bfloat16),
            pltpu.VMEM((features + rows, rows), jnp.float32),
            semaphores, semaphores, semaphores,
        ],
        compiler_params=pltpu.CompilerParams(vmem_limit_bytes=VMEM_LIMIT),
        cost_estimate=pl.CostEstimate(
            flops=2 * rows * columns * (rows + 2 * features),
            bytes_accessed=2 * columns * (rows + 2 * features), transcendentals=0),
        name="late_window",
    )(hidden, base, targets)


OUTER_PARTS = 4


def outer_kernel(place, received, momentum, weights, shard, momentum_out, copies, rs, ms, ws, os_,
                 in_sem, state_sem, copy_sem, out_sem):
    groups, features, width = received.shape
    part_rows = features // OUTER_PARTS
    begin = pl.multiple_of(place[0] * width, 128)
    state = [
        pltpu.make_async_copy(momentum, ms, state_sem.at[0]),
        pltpu.make_async_copy(weights.at[:, pl.ds(begin, width)], ws, state_sem.at[1]),
    ]
    loads = [
        pltpu.make_async_copy(
            received.at[:, pl.ds(part * part_rows, part_rows)],
            rs.at[:, pl.ds(part * part_rows, part_rows)], in_sem.at[part])
        for part in range(OUTER_PARTS)
    ]
    for load in state + loads:
        load.start()
    for load in state:
        load.wait()
    stores = []
    for part in range(OUTER_PARTS):
        rows = pl.ds(part * part_rows, part_rows)
        loads[part].wait()
        total = rs[0, rows].astype(jnp.float32)
        for group in range(1, groups):
            total += rs[group, rows].astype(jnp.float32)
        average = total / groups
        fresh = momentum_rate * ms[rows] + average
        ms[rows] = fresh
        os_[rows] = (
            ws[rows].astype(jnp.float32) - outer_rate * (average + momentum_rate * fresh)
        ).astype(jnp.bfloat16)
        stores += [
            pltpu.make_async_copy(os_.at[rows], copies.at[group, rows], copy_sem.at[part, group])
            for group in range(groups)
        ]
        stores += [
            pltpu.make_async_copy(os_.at[rows], shard.at[rows], out_sem.at[0, part]),
            pltpu.make_async_copy(ms.at[rows], momentum_out.at[rows], out_sem.at[1, part]),
        ]
        for store in stores[-groups - 2:]:
            store.start()
    for store in stores:
        store.wait()


def outer_step(place, received, momentum, weights):
    groups, features, width = received.shape
    anywhere = pl.BlockSpec(memory_space=pl.ANY)
    return pl.pallas_call(
        outer_kernel,
        out_shape=(
            pltpu.HBM(momentum.shape, jnp.bfloat16),
            pltpu.HBM(momentum.shape, jnp.float32),
            pltpu.HBM(received.shape, jnp.bfloat16),
        ),
        in_specs=[pl.BlockSpec(memory_space=pltpu.SMEM)] + [anywhere] * 3,
        out_specs=(anywhere,) * 3,
        scratch_shapes=[
            pltpu.VMEM(received.shape, jnp.bfloat16),
            pltpu.VMEM((features, width), jnp.float32),
            pltpu.VMEM((features, width), jnp.bfloat16),
            pltpu.VMEM((features, width), jnp.bfloat16),
            pltpu.SemaphoreType.DMA((OUTER_PARTS,)),
            pltpu.SemaphoreType.DMA((2,)),
            pltpu.SemaphoreType.DMA((OUTER_PARTS, groups)),
            pltpu.SemaphoreType.DMA((2, OUTER_PARTS)),
        ],
        compiler_params=pltpu.CompilerParams(vmem_limit_bytes=VMEM_LIMIT),
        cost_estimate=pl.CostEstimate(
            flops=groups * features * width, bytes_accessed=4 * groups * features * width,
            transcendentals=0),
        name="outer_step",
    )(place, received, momentum, weights)


def mix_kernel(late, outer, out, late_part, outer_part, mixed, late_sem, outer_sem, out_sem):
    count, _, width = outer.shape

    def columns(piece):
        return pl.ds(piece * width, width)

    loads, stores = [], []
    for piece in range(count):
        loads.append((
            pltpu.make_async_copy(
                late.at[:, columns(piece)], late_part.at[piece], late_sem.at[piece]),
            pltpu.make_async_copy(outer.at[piece], outer_part.at[piece], outer_sem.at[piece])))
        stores.append(pltpu.make_async_copy(
            mixed.at[piece], out.at[:, columns(piece)], out_sem.at[piece]))
        for load in loads[-1]:
            load.start()
    for piece in range(count):
        for load in loads[piece]:
            load.wait()
        mixed[piece] = (
            mixing * late_part[piece].astype(jnp.float32)
            + (1.0 - mixing) * outer_part[piece].astype(jnp.float32)
        ).astype(jnp.bfloat16)
        stores[piece].start()
    for store in stores:
        store.wait()


def mix(late, outer):
    features, columns = late.shape
    anywhere = pl.BlockSpec(memory_space=pl.ANY)
    held = pltpu.VMEM(outer.shape, jnp.bfloat16)
    semaphores = pltpu.SemaphoreType.DMA((PIECES,))
    return pl.pallas_call(
        mix_kernel,
        out_shape=pltpu.HBM((features, columns), jnp.bfloat16),
        in_specs=[anywhere] * 2,
        out_specs=anywhere,
        scratch_shapes=[held] * 3 + [semaphores] * 3,
        compiler_params=pltpu.CompilerParams(vmem_limit_bytes=VMEM_LIMIT),
        cost_estimate=pl.CostEstimate(
            flops=3 * features * columns, bytes_accessed=6 * features * columns,
            transcendentals=0),
        name="mix",
    )(late, outer)


def in_hbm(x):
    return pltpu.with_memory_space_constraint(x, pltpu.HBM)


def body(weights, momentum, hidden, targets):
    features, columns = weights.shape
    width = columns // PIECES
    lanes = lax.axis_size("y")
    depth = lax.axis_size("z")
    cores = lax.axis_size("core")
    own = hidden.reshape(BEFORE + DURING, PIECES, width)

    def near_rows(part, steps):
        return lax.all_gather(part.reshape(steps * PIECES, width), "y", axis=0, tiled=True)

    def target_columns(part, steps):
        parts = part.reshape(steps, depth, lanes, cores, features)
        return parts.transpose(4, 1, 3, 2, 0).reshape(features, -1)

    early_near = near_rows(own[:BEFORE], BEFORE).reshape(2 * lanes * BEFORE, columns // 2)
    early_hidden = lax.all_gather(early_near, RING, axis=0, tiled=True)
    late_near = near_rows(own[BEFORE:], DURING).reshape(lanes * DURING, columns)
    late_hidden = lax.all_gather(late_near, RING, axis=0, tiled=True)
    early_targets = jnp.repeat(target_columns(targets[0, :BEFORE], BEFORE), 2, axis=1)
    late_targets = target_columns(targets[0, BEFORE:], DURING)

    encoded = early_window(BEFORE, early_hidden, weights, early_targets)

    def swap(x):
        return in_hbm(lax.all_to_all(x, REPLICA, split_axis=0, concat_axis=0, tiled=True))

    place = lax.axis_index(REPLICA).astype(jnp.int32)[None]
    outer_shard, momentum_out, copies = outer_step(place, swap(encoded), momentum, weights)
    outer = swap(copies)

    pieces = weights.reshape(features, PIECES, width).transpose(1, 0, 2).astype(jnp.float32)
    base = (pieces - encoded.astype(jnp.float32)).astype(jnp.bfloat16)
    late = late_window(DURING, late_hidden, in_hbm(base), late_targets)
    new_weights = mix(in_hbm(late), outer)[None]
    return (new_weights, outer_shard, momentum_out)


def solution(mesh):
    fine = Mesh(mesh.devices.reshape(8, 4, 2, 2, 4), MESH_AXES)
    placed = (
        P(FSDP, None),
        P(FSDP, REPLICA),
        P(REPLICA, None, FSDP, None),
        P(REPLICA, None, None, FSDP),
    )
    return jax.shard_map(
        body,
        mesh=fine,
        in_specs=placed,
        out_specs=(P(REPLICA, FSDP, None), P(FSDP, REPLICA), P(FSDP, REPLICA)),
        check_vma=False,
    )
```

time: 735 us -> 156 us (0.21)
  waiting for transfers between devices: 655 us -> 70.3 us
  matrix products: 54.2 us -> 0 us
  blocking collectives: 0 us -> 29.1 us
  Pallas kernels: 0 us -> 22.1 us
  starting transfers between devices: 0.53 us -> 9.47 us
    all_gather x8 -> x2, waiting for transfers between devices: 616 us -> 42.5 us  [the longest x1 38.2 us: body(): early_hidden = lax.all_gather(early_near, RING, axis=0, tiled=True)]
    dot_general x7 -> x0, matrix products: 54.2 us -> none  [advance(): lax.dot_general(residual, hidden_rows, (((0,), (0,)), ((), ())), preferre...]
    reduce_scatter x1 -> x0, waiting for transfers between devices: 35.8 us -> none  [synchronize(): lax.psum_scatter(encoded.astype(jnp.float32).astype(jnp.bfloat16), 'repli...]
    all_gather x0 -> x2, blocking collectives: none -> 29.1 us  [near_rows(): lax.all_gather(part.reshape(steps * PIECES, width), 'y', axis=0, tiled=True)]
    all_to_all x0 -> x2, waiting for transfers between devices: none -> 27.8 us  [swap(): lax.all_to_all(x, REPLICA, split_axis=0, concat_axis=0, tiled=True)]
    pallas_call x0 -> x4, Pallas kernels: none -> 22.1 us  [the longest x1 8.13 us: late_window(): pl.pallas_call(functools.partial(late_kernel, steps), out_shape=pltpu.HBM...]
    all_to_all x0 -> x2, starting transfers between devices: none -> 9.39 us  [swap(): lax.all_to_all(x, REPLICA, split_axis=0, concat_axis=0, tiled=True)]
  transfers between devices with their start and end apart: 9 -> 4, of which waited for: 9 -> 4; matrix products, arithmetic and copies ran while one was open for 6% -> 5% of each run, Pallas kernels for 0% -> 12%
where the time goes in v3:
time: 156 us; the launch traced here: 155 us
  waiting for transfers between devices  70.3 us (45%)
  blocking collectives  29.1 us (19%)
  Pallas kernels  22.1 us (14%)
  between operations  14.2 us (9%)
  starting transfers between devices  9.47 us (6%)
  other arithmetic  6.45 us (4%)
  local copies, waits for them, and re-layouts  3.61 us (2%)
    all_gather x1, waiting for transfers between devices, body(): early_hidden = lax.all_gather(early_near, RING, axis=0, tiled=True)  38.2 us
    all_gather x2, blocking collectives, near_rows(): lax.all_gather(part.reshape(steps * PIECES, width), 'y', axis=0, tiled=True)  29.1 us
    all_to_all x2, waiting for transfers between devices, swap(): lax.all_to_all(x, REPLICA, split_axis=0, concat_axis=0, tiled=True)  27.8 us
    all_to_all x2, starting transfers between devices, swap(): lax.all_to_all(x, REPLICA, split_axis=0, concat_axis=0, tiled=True)  9.39 us
    pallas_call x1, Pallas kernels, late_window(): pl.pallas_call(functools.partial(late_kernel, steps), out_shape=pltpu.HBM...  8.13 us
    pallas_call x1, Pallas kernels, early_window(): pl.pallas_call(functools.partial(early_kernel, steps), out_shape=pltpu.HB...  7.51 us
    all_gather x1, waiting for transfers between devices, body(): late_hidden = lax.all_gather(late_near, RING, axis=0, tiled=True)  4.31 us
    convert_element_type x1, other arithmetic, body(): base = (pieces - encoded.astype(jnp.float32)).astype(jnp.bfloat16)  4.3 us
  transfers between devices with their start and end apart: 4, of which 4 were waited for; matrix products, arithmetic and copies ran while one was open for 5% of the time, Pallas kernels for 12%

profile of v3, /device:TPU:1, one launch (start us, length us, event | category | flops | bytes accessed | tf_op | source)
XLA Modules:
  0.0 155.3 jit_solution(2872297107049819549)
XLA Ops:
  7.2 1.0 slice.15
  8.2 0.1 reshape.37
  8.4 16.0 %all_gather.14 = bf16[96,1792]{1,0:T(8,128)(2,1)S(1)} all-gather(bf16[24,1792]{1,0:T(8,128)(2,1)S(1)} %reshape.37), channel_id=1, replica_groups=mesh['z'=8,'y'=4,'core'=2,'y_lo'=2,'x'=4] {'y'}, dimensions={0}, use_global_device_ids=true | all-gather | bytes 430080 | tf_op jit(solution)/shard_map/all_gather | solution.py:364
  24.3 1.0 reshape.38
  25.4 0.1 slice.14
  25.4 0.1 reshape.35
  25.5 13.2 %all_gather.12 = bf16[128,1792]{1,0:T(8,128)(2,1)S(1)} all-gather(bf16[32,1792]{1,0:T(8,128)(2,1)S(1)} %reshape.35), channel_id=1, replica_groups=mesh['z'=8,'y'=4,'core'=2,'y_lo'=2,'x'=4] {'y'}, dimensions={0}, use_global_device_ids=true | all-gather | bytes 573440 | tf_op jit(solution)/shard_map/all_gather | solution.py:364
  38.7 1.0 reshape.36
  39.8 0.1 broadcast_in_dim.9
  39.9 0.1 copy.10.targets
  40.0 38.2 %all-gather.5.cloned.1.call-done.hidden = bf16[384,7168]{1,0:T(8,128)(2,1)} async-done(((bf16[24,7168]{1,0:T(8,128)(2,1)}), bf16[384,7168]{1,0:T(8,128)(2,1)}) %all-gather.5.cloned.1.call-update) | async-done | bytes 5505040 | tf_op jit(solution)/shard_map/all_gather | solution.py:371
  78.2 7.5 %early_window.1 = bf16[8,64,1792]{2,1,0:T(8,128)(2,1)} custom-call(bf16[384,7168]{1,0:T(8,128)(2,1)} %all-gather.5.cloned.1.call-done.hidden, bf16[64,14336]{1,0:T(8,128)(2,1)S(1)} %copy-done, bf16[64,384]{1,0:T(8,128)(2,1)S(1)} %copy.10.targets), custom_call_target="tpu_custom_call" | custom-call | flops 3523215360 | bytes 9175040 | tf_op jit(solution)/shard_map/early_window/pallas_call | solution.py:132
  85.7 5.0 %all-to-all-start = ((bf16[8,64,1792]{2,1,0:T(8,128)(2,1)}), bf16[8,64,1792]{2,1,0:T(8,128)(2,1)}, u32[]{:S(2)}, u32[]{:S(2)}) async-start(bf16[8,64,1792]{2,1,0:T(8,128)(2,1)} %early_window.1), calls=%async_computation | async-start | bytes 3670016 | tf_op jit(solution)/shard_map/all_to_all | solution.py:380
  90.8 23.5 %all-to-all-done.received = bf16[8,64,1792]{2,1,0:T(8,128)(2,1)} async-done(((bf16[8,64,1792]{2,1,0:T(8,128)(2,1)}), bf16[8,64,1792]{2,1,0:T(8,128)(2,1)}, u32[]{:S(2)}, u32[]{:S(2)}) %all-to-all-start) | async-done | bytes 1835040 | tf_op jit(solution)/shard_map/all_to_all | solution.py:380
  114.3 3.2 %outer_step.1 = (bf16[64,1792]{1,0:T(8,128)(2,1)}, f32[64,1792]{1,0:T(8,128)}, bf16[8,64,1792]{2,1,0:T(8,128)(2,1)}) custom-call(s32[1]{0:T(128)} %bitcast.7.place, bf16[8,64,1792]{2,1,0:T(8,128)(2,1)} %all-to-all-done.received, f32[64,1792]{1,0:T(8,128)S(1)} %copy-done.1, bf16[64,14336]{1,0:T(8,128)(2,1)S(1)} %copy-done), custom_call_target="tpu_custom_call" | custom-call | flops 917504 | bytes 3670016 | tf_op jit(solution)/shard_map/outer_step/pallas_call | solution.py:277
  117.5 4.3 %all-to-all-start.1 = ((bf16[8,64,1792]{2,1,0:T(8,128)(2,1)}), bf16[8,64,1792]{2,1,0:T(8,128)(2,1)}, u32[]{:S(2)}, u32[]{:S(2)}) async-start(bf16[8,64,1792]{2,1,0:T(8,128)(2,1)} %get-tuple-element.6), calls=%async_computation.1 | async-start | bytes 3670016 | tf_op jit(solution)/shard_map/all_to_all | solution.py:380
  121.9 2.1 %convert_element_type.21 = f32[64,14336]{1,0:T(8,128)} convert(bf16[64,14336]{1,0:T(8,128)(2,1)S(1)} %copy-done) | non-fusion elementwise | flops 917504 | bytes 5505024 | tf_op jit(solution)/shard_map/convert_element_type | solution.py:386
  124.0 0.1 copy.11
  124.1 0.1 copy.12.targets
  124.2 4.3 %fusion.1.base = bf16[8,64,1792]{2,1,0:T(8,128)(2,1)} fusion(f32[8,8,8,1792]{3,2,1,0:T(8,128)} %bitcast.30, bf16[8,64,1792]{2,1,0:T(8,128)(2,1)} %early_window.1), kind=kLoop, calls=%fused_computation.2 | loop fusion | flops 2752512 | bytes 7340032 | tf_op jit(solution)/shard_map/convert_element_type | solution.py:387
  128.5 4.3 %all-gather.3.cloned.1.call-done.hidden = bf16[256,14336]{1,0:T(8,128)(2,1)} async-done(((bf16[16,14336]{1,0:T(8,128)(2,1)}), bf16[256,14336]{1,0:T(8,128)(2,1)}) %all-gather.3.cloned.1.call-update) | async-done | bytes 7340048 | tf_op jit(solution)/shard_map/all_gather | solution.py:373
  132.8 8.1 %late_window.1.late = bf16[64,14336]{1,0:T(8,128)(2,1)} custom-call(bf16[256,14336]{1,0:T(8,128)(2,1)} %all-gather.3.cloned.1.call-done.hidden, bf16[8,64,1792]{2,1,0:T(8,128)(2,1)} %fusion.1.base, bf16[64,256]{1,0:T(8,128)(2,1)S(1)} %copy.12.targets), custom_call_target="tpu_custom_call" | custom-call | flops 2818572288 | bytes 11010048 | tf_op jit(solution)/shard_map/late_window/pallas_call | solution.py:206
  140.9 4.3 %all-to-all-done.1.outer = bf16[8,64,1792]{2,1,0:T(8,128)(2,1)} async-done(((bf16[8,64,1792]{2,1,0:T(8,128)(2,1)}), bf16[8,64,1792]{2,1,0:T(8,128)(2,1)}, u32[]{:S(2)}, u32[]{:S(2)}) %all-to-all-start.1) | async-done | bytes 1835040 | tf_op jit(solution)/shard_map/all_to_all | solution.py:380
  145.2 3.2 %mix.1 = bf16[64,14336]{1,0:T(8,128)(2,1)} custom-call(bf16[64,14336]{1,0:T(8,128)(2,1)} %late_window.1.late, bf16[8,64,1792]{2,1,0:T(8,128)(2,1)} %all-to-all-done.1.outer), custom_call_target="tpu_custom_call" | custom-call | flops 2752512 | bytes 5505024 | tf_op jit(solution)/shard_map/mix/pallas_call | solution.py:337
  (16 shorter events, 0.2 us)
Async XLA Ops:
  7.2 18.2 %copy-start.2 = (bf16[1,7,1,14336]{3,1,2,0:T(8,128)(2,1)S(1)}, bf16[1,7,1,14336]{3,1,2,0:T(8,128)(2,1)}, u32[]{:S(2)}) copy-start(bf16[1,7,1,14336]{3,1,2,0:T(8,128)(2,1)} %param.6) | copy-start | bytes 602116
  7.2 71.0 %all-gather.5.cloned.1.call-start = ((), (), s32[]{:S(2)}) async-start(), calls=%async_computation.3 | async-start | bytes 5849088 | tf_op jit(solution)/shard_map/all_gather | solution.py:371
  24.3 15.4 %slice-start = ((bf16[1,7,64,64]{3,2,1,0:T(8,128)(2,1)}), bf16[1,3,64,64]{3,2,1,0:T(8,128)(2,1)S(1)}, s32[]{:S(2)}) async-start(bf16[1,7,64,64]{3,2,1,0:T(8,128)(2,1)} %param.7), calls=%async_computation.4 | async-start | bytes 98304 | tf_op jit(solution)/shard_map/slice | solution.py:374
  25.3 52.9 %copy-start = (bf16[64,14336]{1,0:T(8,128)(2,1)S(1)}, bf16[64,14336]{1,0:T(8,128)(2,1)}, u32[]{:S(2)}) copy-start(bf16[64,14336]{1,0:T(8,128)(2,1)} %weights.3) | copy-start | bytes 5505028
  25.3 107.5 %all-gather.3.cloned.1.call-start = ((), (), s32[]{:S(2)}) async-start(), calls=%async_computation.2 | async-start | bytes 7798784 | tf_op jit(solution)/shard_map/all_gather | solution.py:373
  85.7 28.6 %copy-start.1 = (f32[64,1792]{1,0:T(8,128)S(1)}, f32[64,1792]{1,0:T(8,128)}, u32[]{:S(2)}) copy-start(f32[64,1792]{1,0:T(8,128)} %momentum.1) | copy-start | bytes 1376260
  85.7 28.5 %all-to-all-start = ((bf16[8,64,1792]{2,1,0:T(8,128)(2,1)}), bf16[8,64,1792]{2,1,0:T(8,128)(2,1)}, u32[]{:S(2)}, u32[]{:S(2)}) async-start(bf16[8,64,1792]{2,1,0:T(8,128)(2,1)} %early_window.1), calls=%async_computation | async-start | bytes 3670016 | tf_op jit(solution)/shard_map/all_to_all | solution.py:380
  117.5 27.7 %all-to-all-start.1 = ((bf16[8,64,1792]{2,1,0:T(8,128)(2,1)}), bf16[8,64,1792]{2,1,0:T(8,128)(2,1)}, u32[]{:S(2)}, u32[]{:S(2)}) async-start(bf16[8,64,1792]{2,1,0:T(8,128)(2,1)} %get-tuple-element.6), calls=%async_computation.1 | async-start | bytes 3670016 | tf_op jit(solution)/shard_map/all_to_all | solution.py:380
  121.9 2.2 %slice-start.1 = ((bf16[1,7,64,64]{3,2,1,0:T(8,128)(2,1)}), bf16[1,4,64,64]{3,2,1,0:T(8,128)(2,1)S(1)}, s32[]{:S(2)}) async-start(bf16[1,7,64,64]{3,2,1,0:T(8,128)(2,1)} %param.7), calls=%async_computation.5 | async-start | bytes 131072 | tf_op jit(solution)/shard_map/slice | solution.py:375
Sparse Core Ops, SparseCore 0:
  25.4 52.7 all-gather.4
  80.3 52.4 all-gather.2

commit v4 on v3

--- a/solution.py
+++ b/solution.py
@@ -24,10 +24,12 @@
 PIECES = 8
 VMEM_LIMIT = 48 * 1024 * 1024
 AHEAD = 3
+EARLY_PIECE = 1536
+EARLY_COUNT = 8
 ACROSS = (((1,), (1,)), ((), ()))
 
 
-def in_order(count, start, use, unroll):
+def in_order(count, start, use):
     for piece in range(min(AHEAD, count)):
         start(piece)
 
@@ -39,7 +41,7 @@
         use(piece)
         return carry
 
-    lax.fori_loop(0, count, turn, 0, unroll=unroll)
+    lax.fori_loop(0, count, turn, 0)
 
 
 def solve(steps, step_of, scaled, gram, wanted, moved_by, total):
@@ -58,38 +60,54 @@
     return residual
 
 
-def early_kernel(steps, hidden, weights, targets, out, held, outs, both_ref, hidden_sem,
-                 weights_sem, out_sem):
-    rows = hidden.shape[0]
-    count, _, width = held.shape
-    features = weights.shape[0]
+def early_kernel(steps, parts, *refs):
+    hidden = refs[:parts]
+    weights, targets, out, held, outs, both_ref, hidden_sem, weights_sem, out_sem = refs[parts:]
+    rows = hidden[0].shape[0]
+    half = held.shape[1]
+    features, columns = weights.shape
     top = 2 * features
-    inverse_root = 1.0 / math.sqrt(weights.shape[1])
-
-    def copies(piece):
+    width = columns // PIECES
+    inverse_root = 1.0 / math.sqrt(columns)
+
+    pieces, begin = [], 0
+    for part in range(parts):
+        size = hidden[part].shape[1]
+        cuts = 1 if size <= EARLY_PIECE else size // EARLY_PIECE
+        for cut in range(cuts):
+            pieces.append((part, cut * (size // cuts), begin, size // cuts))
+            begin += size // cuts
+
+    def copies(number):
+        part, first, place, size = pieces[number]
         yield pltpu.make_async_copy(
-            hidden.at[:, pl.ds(piece * width, width)], held.at[piece, pl.ds(top, rows)],
-            hidden_sem.at[piece])
+            hidden[part].at[:, pl.ds(first, size)],
+            held.at[pl.ds(top, rows), pl.ds(place, size)], hidden_sem.at[number])
         for side in range(2):
             yield pltpu.make_async_copy(
-                weights.at[:, pl.ds((side * count + piece) * width, width)],
-                held.at[piece, pl.ds(side * features, features)], weights_sem.at[side, piece])
+                weights.at[:, pl.ds(side * half + place, size)],
+                held.at[pl.ds(side * features, features), pl.ds(place, size)],
+                weights_sem.at[side, number])
 
     def out_copy(piece):
         return pltpu.make_async_copy(outs.at[piece], out.at[piece], out_sem.at[piece])
 
-    def start(piece):
-        for copy in copies(piece):
+    def start(number):
+        for copy in copies(number):
             copy.start()
 
-    def products(piece):
-        for copy in copies(piece):
+    for number in range(min(AHEAD, len(pieces))):
+        start(number)
+    for number, (_, _, place, size) in enumerate(pieces):
+        if number + AHEAD < len(pieces):
+            start(number + AHEAD)
+        for copy in copies(number):
             copy.wait()
-        both_ref[...] += lax.dot_general(
-            held[piece, top:], held[piece], ACROSS, preferred_element_type=jnp.float32)
-
-    both_ref[...] = jnp.zeros_like(both_ref)
-    in_order(count, start, products, count)
+        block = pl.ds(place, size)
+        product = lax.dot_general(
+            held[pl.ds(top, rows), block], held[:, block], ACROSS,
+            preferred_element_type=jnp.float32)
+        both_ref[...] = product if number == 0 else both_ref[...] + product
 
     column = lax.broadcasted_iota(jnp.int32, (features, rows), 1)
     left = column % 2 == 0
@@ -108,38 +126,36 @@
         [jnp.where(left, residual, 0.0), jnp.where(left, 0.0, residual)], axis=0
     ).astype(jnp.bfloat16)
 
-    def write(piece, carry):
+    count = half // width
+    for piece in range(count):
         update = (inner_rate * inverse_root) * jnp.dot(
-            factors, held[piece, top:], preferred_element_type=jnp.float32)
+            factors, held[pl.ds(top, rows), pl.ds(piece * width, width)],
+            preferred_element_type=jnp.float32)
         encoded = update.astype(jnp.bfloat16)
         outs[piece] = encoded[:features]
         outs[count + piece] = encoded[features:]
         out_copy(piece).start()
         out_copy(count + piece).start()
-        return carry
-
-    lax.fori_loop(0, count, write, 0, unroll=4)
     for piece in range(PIECES):
         out_copy(piece).wait()
 
 
 def early_window(steps, hidden, weights, targets):
-    rows = hidden.shape[0]
+    rows = hidden[0].shape[0]
     features, columns = weights.shape
     width = columns // PIECES
-    count = PIECES // 2
     anywhere = pl.BlockSpec(memory_space=pl.ANY)
     return pl.pallas_call(
-        functools.partial(early_kernel, steps),
+        functools.partial(early_kernel, steps, len(hidden)),
         out_shape=pltpu.HBM((PIECES, features, width), jnp.bfloat16),
-        in_specs=[anywhere, anywhere, pl.BlockSpec(memory_space=pltpu.VMEM)],
+        in_specs=[anywhere] * (len(hidden) + 1) + [pl.BlockSpec(memory_space=pltpu.VMEM)],
         out_specs=anywhere,
         scratch_shapes=[
-            pltpu.VMEM((count, 2 * features + rows, width), jnp.bfloat16),
+            pltpu.VMEM((2 * features + rows, columns // 2), jnp.bfloat16),
             pltpu.VMEM((PIECES, features, width), jnp.bfloat16),
             pltpu.VMEM((rows, 2 * features + rows), jnp.float32),
-            pltpu.SemaphoreType.DMA((count,)),
-            pltpu.SemaphoreType.DMA((2, count)),
+            pltpu.SemaphoreType.DMA((EARLY_COUNT,)),
+            pltpu.SemaphoreType.DMA((2, EARLY_COUNT)),
             pltpu.SemaphoreType.DMA((PIECES,)),
         ],
         compiler_params=pltpu.CompilerParams(vmem_limit_bytes=VMEM_LIMIT),
@@ -147,7 +163,7 @@
             flops=rows * columns * (rows + 4 * features),
             bytes_accessed=columns * (rows + 4 * features), transcendentals=0),
         name="early_window",
-    )(hidden, weights, targets)
+    )(*hidden, weights, targets)
 
 
 def late_kernel(steps, hidden, base, targets, out, held, outs, both_ref, hidden_sem, base_sem,
@@ -178,7 +194,7 @@
             held[piece], held[piece, features:], ACROSS, preferred_element_type=jnp.float32)
 
     both_ref[...] = jnp.zeros_like(both_ref)
-    in_order(count, start, products, 1)
+    in_order(count, start, products)
 
     step_of = lax.broadcasted_iota(jnp.int32, (features, rows), 1) % steps
     residual = solve(steps, step_of, both_ref[:features] * inverse_root, both_ref[features:],
@@ -225,37 +241,22 @@
 OUTER_PARTS = 4
 
 
-def outer_kernel(place, received, momentum, weights, shard, momentum_out, copies, rs, ms, ws, os_,
-                 in_sem, state_sem, copy_sem, out_sem):
+def outer_kernel(received, momentum, rows_before, shard, momentum_out, copies, ms, os_, copy_sem,
+                 out_sem):
     groups, features, width = received.shape
     part_rows = features // OUTER_PARTS
-    begin = pl.multiple_of(place[0] * width, 128)
-    state = [
-        pltpu.make_async_copy(momentum, ms, state_sem.at[0]),
-        pltpu.make_async_copy(weights.at[:, pl.ds(begin, width)], ws, state_sem.at[1]),
-    ]
-    loads = [
-        pltpu.make_async_copy(
-            received.at[:, pl.ds(part * part_rows, part_rows)],
-            rs.at[:, pl.ds(part * part_rows, part_rows)], in_sem.at[part])
-        for part in range(OUTER_PARTS)
-    ]
-    for load in state + loads:
-        load.start()
-    for load in state:
-        load.wait()
     stores = []
     for part in range(OUTER_PARTS):
         rows = pl.ds(part * part_rows, part_rows)
-        loads[part].wait()
-        total = rs[0, rows].astype(jnp.float32)
+        total = received[0, rows].astype(jnp.float32)
         for group in range(1, groups):
-            total += rs[group, rows].astype(jnp.float32)
+            total += received[group, rows].astype(jnp.float32)
         average = total / groups
-        fresh = momentum_rate * ms[rows] + average
+        fresh = momentum_rate * momentum[rows] + average
         ms[rows] = fresh
         os_[rows] = (
-            ws[rows].astype(jnp.float32) - outer_rate * (average + momentum_rate * fresh)
+            rows_before[rows].astype(jnp.float32)
+            - outer_rate * (average + momentum_rate * fresh)
         ).astype(jnp.bfloat16)
         stores += [
             pltpu.make_async_copy(os_.at[rows], copies.at[group, rows], copy_sem.at[part, group])
@@ -271,7 +272,7 @@
         store.wait()
 
 
-def outer_step(place, received, momentum, weights):
+def outer_step(received, momentum, rows_before):
     groups, features, width = received.shape
     anywhere = pl.BlockSpec(memory_space=pl.ANY)
     return pl.pallas_call(
@@ -281,15 +282,11 @@
             pltpu.HBM(momentum.shape, jnp.float32),
             pltpu.HBM(received.shape, jnp.bfloat16),
         ),
-        in_specs=[pl.BlockSpec(memory_space=pltpu.SMEM)] + [anywhere] * 3,
+        in_specs=[pl.BlockSpec(memory_space=pltpu.VMEM)] * 3,
         out_specs=(anywhere,) * 3,
         scratch_shapes=[
-            pltpu.VMEM(received.shape, jnp.bfloat16),
             pltpu.VMEM((features, width), jnp.float32),
             pltpu.VMEM((features, width), jnp.bfloat16),
-            pltpu.VMEM((features, width), jnp.bfloat16),
-            pltpu.SemaphoreType.DMA((OUTER_PARTS,)),
-            pltpu.SemaphoreType.DMA((2,)),
             pltpu.SemaphoreType.DMA((OUTER_PARTS, groups)),
             pltpu.SemaphoreType.DMA((2, OUTER_PARTS)),
         ],
@@ -298,10 +295,10 @@
             flops=groups * features * width, bytes_accessed=4 * groups * features * width,
             transcendentals=0),
         name="outer_step",
-    )(place, received, momentum, weights)
-
-
-def mix_kernel(late, outer, out, late_part, outer_part, mixed, late_sem, outer_sem, out_sem):
+    )(received, momentum, rows_before)
+
+
+def mix_kernel(late, outer, out, late_part, mixed, late_sem, out_sem):
     count, _, width = outer.shape
 
     def columns(piece):
@@ -309,20 +306,16 @@
 
     loads, stores = [], []
     for piece in range(count):
-        loads.append((
-            pltpu.make_async_copy(
-                late.at[:, columns(piece)], late_part.at[piece], late_sem.at[piece]),
-            pltpu.make_async_copy(outer.at[piece], outer_part.at[piece], outer_sem.at[piece])))
+        loads.append(pltpu.make_async_copy(
+            late.at[:, columns(piece)], late_part.at[piece], late_sem.at[piece]))
         stores.append(pltpu.make_async_copy(
             mixed.at[piece], out.at[:, columns(piece)], out_sem.at[piece]))
-        for load in loads[-1]:
-            load.start()
+        loads[-1].start()
     for piece in range(count):
-        for load in loads[piece]:
-            load.wait()
+        loads[piece].wait()
         mixed[piece] = (
             mixing * late_part[piece].astype(jnp.float32)
-            + (1.0 - mixing) * outer_part[piece].astype(jnp.float32)
+            + (1.0 - mixing) * outer[piece].astype(jnp.float32)
         ).astype(jnp.bfloat16)
         stores[piece].start()
     for store in stores:
@@ -337,9 +330,9 @@
     return pl.pallas_call(
         mix_kernel,
         out_shape=pltpu.HBM((features, columns), jnp.bfloat16),
-        in_specs=[anywhere] * 2,
+        in_specs=[anywhere, pl.BlockSpec(memory_space=pltpu.VMEM)],
         out_specs=anywhere,
-        scratch_shapes=[held] * 3 + [semaphores] * 3,
+        scratch_shapes=[held] * 2 + [semaphores] * 2,
         compiler_params=pltpu.CompilerParams(vmem_limit_bytes=VMEM_LIMIT),
         cost_estimate=pl.CostEstimate(
             flops=3 * features * columns, bytes_accessed=6 * features * columns,
@@ -374,13 +367,14 @@
     early_targets = jnp.repeat(target_columns(targets[0, :BEFORE], BEFORE), 2, axis=1)
     late_targets = target_columns(targets[0, BEFORE:], DURING)
 
-    encoded = early_window(BEFORE, early_hidden, weights, early_targets)
+    encoded = early_window(BEFORE, [early_hidden], weights, early_targets)
 
     def swap(x):
-        return in_hbm(lax.all_to_all(x, REPLICA, split_axis=0, concat_axis=0, tiled=True))
-
-    place = lax.axis_index(REPLICA).astype(jnp.int32)[None]
-    outer_shard, momentum_out, copies = outer_step(place, swap(encoded), momentum, weights)
+        return lax.all_to_all(x, REPLICA, split_axis=0, concat_axis=0, tiled=True)
+
+    rows_before = lax.dynamic_slice_in_dim(
+        weights, lax.axis_index(REPLICA) * width, width, 1)
+    outer_shard, momentum_out, copies = outer_step(swap(encoded), momentum, rows_before)
     outer = swap(copies)
 
     pieces = weights.reshape(features, PIECES, width).transpose(1, 0, 2).astype(jnp.float32)

time: 156 us -> 153 us (0.981)
  waiting for transfers between devices: 70.3 us -> 67.7 us
  Pallas kernels: 22.1 us -> 20.2 us
  other arithmetic: 6.45 us -> 8.1 us
    all_to_all x2, waiting for transfers between devices: 27.8 us -> 24.8 us  [swap(): return lax.all_to_all(x, REPLICA, split_axis=0, concat_axis=0, tiled=True)]
    convert_element_type x1, other arithmetic: 2.15 us -> 3.75 us  [body(): weights.reshape(features, PIECES, width).transpose(1, 0, 2)]
  transfers between devices with their start and end apart: 4 -> 4, of which waited for: 4 -> 4; matrix products, arithmetic and copies ran while one was open for 5% -> 7% of each run, Pallas kernels for 12% -> 12%
where the time goes in v4:
time: 153 us
  waiting for transfers between devices  67.7 us (44%)
  blocking collectives  29.1 us (19%)
  Pallas kernels  20.2 us (13%)
  between operations  14.2 us (9%)
  starting transfers between devices  8.71 us (6%)
  other arithmetic  8.1 us (5%)
  local copies, waits for them, and re-layouts  4.61 us (3%)
    all_gather x1, waiting for transfers between devices, body(): early_hidden = lax.all_gather(early_near, RING, axis=0, tiled=True)  38.2 us
    all_gather x2, blocking collectives, near_rows(): lax.all_gather(part.reshape(steps * PIECES, width), 'y', axis=0, tiled=True)  29.1 us
    all_to_all x2, waiting for transfers between devices, swap(): return lax.all_to_all(x, REPLICA, split_axis=0, concat_axis=0, tiled=True)  24.8 us
    all_to_all x2, starting transfers between devices, swap(): return lax.all_to_all(x, REPLICA, split_axis=0, concat_axis=0, tiled=True)  8.63 us
    pallas_call x1, Pallas kernels, late_window(): pl.pallas_call(functools.partial(late_kernel, steps), out_shape=pltpu.HBM...  8.13 us
    pallas_call x1, Pallas kernels, early_window(): pl.pallas_call(functools.partial(early_kernel, steps, len(hidden)), out_s...  7.63 us
    all_gather x1, waiting for transfers between devices, body(): late_hidden = lax.all_gather(late_near, RING, axis=0, tiled=True)  4.66 us
    convert_element_type x1, other arithmetic, body(): base = (pieces - encoded.astype(jnp.float32)).astype(jnp.bfloat16)  4.35 us
  transfers between devices with their start and end apart: 4, of which 4 were waited for; matrix products, arithmetic and copies ran while one was open for 7% of the time, Pallas kernels for 12%

profile of v4, /device:TPU:1, one launch (start us, length us, event | category | flops | bytes accessed | tf_op | source)
XLA Modules:
  0.0 152.6 jit_solution(11632823829733486249)
XLA Ops:
  7.2 1.0 slice.15
  8.2 0.1 reshape.37
  8.4 16.0 %all_gather.14 = bf16[96,1792]{1,0:T(8,128)(2,1)S(1)} all-gather(bf16[24,1792]{1,0:T(8,128)(2,1)S(1)} %reshape.37), channel_id=1, replica_groups=mesh['z'=8,'y'=4,'core'=2,'y_lo'=2,'x'=4] {'y'}, dimensions={0}, use_global_device_ids=true | all-gather | bytes 430080 | tf_op jit(solution)/shard_map/all_gather | solution.py:357
  24.3 1.0 reshape.38
  25.4 0.1 slice.14
  25.4 0.1 reshape.35
  25.5 13.2 %all_gather.12 = bf16[128,1792]{1,0:T(8,128)(2,1)S(1)} all-gather(bf16[32,1792]{1,0:T(8,128)(2,1)S(1)} %reshape.35), channel_id=1, replica_groups=mesh['z'=8,'y'=4,'core'=2,'y_lo'=2,'x'=4] {'y'}, dimensions={0}, use_global_device_ids=true | all-gather | bytes 573440 | tf_op jit(solution)/shard_map/all_gather | solution.py:357
  38.7 1.0 reshape.36
  39.9 0.1 broadcast_in_dim.6
  39.9 0.1 copy.10.refs_2_
  40.0 38.2 %all-gather.5.cloned.1.call-done.refs_0_ = bf16[384,7168]{1,0:T(8,128)(2,1)} async-done(((bf16[24,7168]{1,0:T(8,128)(2,1)}), bf16[384,7168]{1,0:T(8,128)(2,1)}) %all-gather.5.cloned.1.call-update) | async-done | bytes 5505040 | tf_op jit(solution)/shard_map/all_gather | solution.py:364
  78.2 7.6 %early_window.1 = bf16[8,64,1792]{2,1,0:T(8,128)(2,1)} custom-call(bf16[384,7168]{1,0:T(8,128)(2,1)} %all-gather.5.cloned.1.call-done.refs_0_, bf16[64,14336]{1,0:T(8,128)(2,1)S(1)} %copy-done, bf16[64,384]{1,0:T(8,128)(2,1)S(1)} %copy.10.refs_2_), custom_call_target="tpu_custom_call" | custom-call | flops 3523215360 | bytes 9175040 | tf_op jit(solution)/shard_map/early_window/pallas_call | solution.py:148
  85.9 5.0 %all-to-all-start = ((bf16[8,64,1792]{2,1,0:T(8,128)(2,1)}), bf16[8,64,1792]{2,1,0:T(8,128)(2,1)S(1)}, u32[]{:S(2)}, u32[]{:S(2)}) async-start(bf16[8,64,1792]{2,1,0:T(8,128)(2,1)} %early_window.1), calls=%async_computation | async-start | bytes 3670016 | tf_op jit(solution)/shard_map/all_to_all | solution.py:373
  90.9 1.0 constant_dynamic-slice_fusion.rows_before
  91.8 22.5 %all-to-all-done.received = bf16[8,64,1792]{2,1,0:T(8,128)(2,1)S(1)} async-done(((bf16[8,64,1792]{2,1,0:T(8,128)(2,1)}), bf16[8,64,1792]{2,1,0:T(8,128)(2,1)S(1)}, u32[]{:S(2)}, u32[]{:S(2)}) %all-to-all-start) | async-done | bytes 1835040 | tf_op jit(solution)/shard_map/all_to_all | solution.py:373
  114.4 1.9 %outer_step.1 = (bf16[64,1792]{1,0:T(8,128)(2,1)}, f32[64,1792]{1,0:T(8,128)}, bf16[8,64,1792]{2,1,0:T(8,128)(2,1)}) custom-call(bf16[8,64,1792]{2,1,0:T(8,128)(2,1)S(1)} %all-to-all-done.received, f32[64,1792]{1,0:T(8,128)S(1)} %copy-done.1, bf16[64,1792]{1,0:T(8,128)(2,1)S(1)} %constant_dynamic-slice_fusion.rows_before), custom_call_target="tpu_custom_call" | custom-call | flops 917504 | bytes 3670016 | tf_op jit(solution)/shard_map/outer_step/pallas_call | solution.py:278
  116.3 3.6 %all-to-all-start.1 = ((bf16[8,64,1792]{2,1,0:T(8,128)(2,1)}), bf16[8,64,1792]{2,1,0:T(8,128)(2,1)S(1)}, u32[]{:S(2)}, u32[]{:S(2)}) async-start(bf16[8,64,1792]{2,1,0:T(8,128)(2,1)} %get-tuple-element.6), calls=%async_computation.1 | async-start | bytes 3670016 | tf_op jit(solution)/shard_map/all_to_all | solution.py:373
  119.9 3.7 %convert_element_type.21 = f32[64,14336]{1,0:T(8,128)} convert(bf16[64,14336]{1,0:T(8,128)(2,1)} %refs_1_.1) | non-fusion elementwise | flops 917504 | bytes 5505024 | tf_op jit(solution)/shard_map/convert_element_type | solution.py:380
  123.7 0.1 copy.12.targets
  123.8 4.3 %fusion.1.base = bf16[8,64,1792]{2,1,0:T(8,128)(2,1)} fusion(f32[8,8,8,1792]{3,2,1,0:T(8,128)} %bitcast.29, bf16[8,64,1792]{2,1,0:T(8,128)(2,1)} %early_window.1), kind=kLoop, calls=%fused_computation.2 | loop fusion | flops 2752512 | bytes 7340032 | tf_op jit(solution)/shard_map/convert_element_type | solution.py:381
  128.1 4.7 %all-gather.3.cloned.1.call-done.hidden = bf16[256,14336]{1,0:T(8,128)(2,1)} async-done(((bf16[16,14336]{1,0:T(8,128)(2,1)}), bf16[256,14336]{1,0:T(8,128)(2,1)}) %all-gather.3.cloned.1.call-update) | async-done | bytes 7340048 | tf_op jit(solution)/shard_map/all_gather | solution.py:366
  132.8 8.1 %late_window.1.late = bf16[64,14336]{1,0:T(8,128)(2,1)} custom-call(bf16[256,14336]{1,0:T(8,128)(2,1)} %all-gather.3.cloned.1.call-done.hidden, bf16[8,64,1792]{2,1,0:T(8,128)(2,1)} %fusion.1.base, bf16[64,256]{1,0:T(8,128)(2,1)S(1)} %copy.12.targets), custom_call_target="tpu_custom_call" | custom-call | flops 2818572288 | bytes 11010048 | tf_op jit(solution)/shard_map/late_window/pallas_call | solution.py:222
  140.9 2.2 %all-to-all-done.1.outer = bf16[8,64,1792]{2,1,0:T(8,128)(2,1)S(1)} async-done(((bf16[8,64,1792]{2,1,0:T(8,128)(2,1)}), bf16[8,64,1792]{2,1,0:T(8,128)(2,1)S(1)}, u32[]{:S(2)}, u32[]{:S(2)}) %all-to-all-start.1) | async-done | bytes 1835040 | tf_op jit(solution)/shard_map/all_to_all | solution.py:373
  143.2 2.5 %mix.1 = bf16[64,14336]{1,0:T(8,128)(2,1)} custom-call(bf16[64,14336]{1,0:T(8,128)(2,1)} %late_window.1.late, bf16[8,64,1792]{2,1,0:T(8,128)(2,1)S(1)} %all-to-all-done.1.outer), custom_call_target="tpu_custom_call" | custom-call | flops 2752512 | bytes 5505024 | tf_op jit(solution)/shard_map/mix/pallas_call | solution.py:330
  (17 shorter events, 0.3 us)
Async XLA Ops:
  7.2 18.2 %copy-start.2 = (bf16[1,7,1,14336]{3,1,2,0:T(8,128)(2,1)S(1)}, bf16[1,7,1,14336]{3,1,2,0:T(8,128)(2,1)}, u32[]{:S(2)}) copy-start(bf16[1,7,1,14336]{3,1,2,0:T(8,128)(2,1)} %param.6) | copy-start | bytes 602116
  7.2 71.0 %all-gather.5.cloned.1.call-start = ((), (), s32[]{:S(2)}) async-start(), calls=%async_computation.3 | async-start | bytes 5849088 | tf_op jit(solution)/shard_map/all_gather | solution.py:364
  24.3 15.4 %slice-start = ((bf16[1,7,64,64]{3,2,1,0:T(8,128)(2,1)}), bf16[1,3,64,64]{3,2,1,0:T(8,128)(2,1)S(1)}, s32[]{:S(2)}) async-start(bf16[1,7,64,64]{3,2,1,0:T(8,128)(2,1)} %param.7), calls=%async_computation.4 | async-start | bytes 98304 | tf_op jit(solution)/shard_map/slice | solution.py:367
  25.3 52.9 %copy-start = (bf16[64,14336]{1,0:T(8,128)(2,1)S(1)}, bf16[64,14336]{1,0:T(8,128)(2,1)}, u32[]{:S(2)}) copy-start(bf16[64,14336]{1,0:T(8,128)(2,1)} %refs_1_.1) | copy-start | bytes 5505028
  25.3 107.5 %all-gather.3.cloned.1.call-start = ((), (), s32[]{:S(2)}) async-start(), calls=%async_computation.2 | async-start | bytes 7798784 | tf_op jit(solution)/shard_map/all_gather | solution.py:366
  85.8 28.5 %copy-start.1 = (f32[64,1792]{1,0:T(8,128)S(1)}, f32[64,1792]{1,0:T(8,128)}, u32[]{:S(2)}) copy-start(f32[64,1792]{1,0:T(8,128)} %momentum.1) | copy-start | bytes 1376260
  85.9 28.5 %all-to-all-start = ((bf16[8,64,1792]{2,1,0:T(8,128)(2,1)}), bf16[8,64,1792]{2,1,0:T(8,128)(2,1)S(1)}, u32[]{:S(2)}, u32[]{:S(2)}) async-start(bf16[8,64,1792]{2,1,0:T(8,128)(2,1)} %early_window.1), calls=%async_computation | async-start | bytes 3670016 | tf_op jit(solution)/shard_map/all_to_all | solution.py:373
  116.3 26.9 %all-to-all-start.1 = ((bf16[8,64,1792]{2,1,0:T(8,128)(2,1)}), bf16[8,64,1792]{2,1,0:T(8,128)(2,1)S(1)}, u32[]{:S(2)}, u32[]{:S(2)}) async-start(bf16[8,64,1792]{2,1,0:T(8,128)(2,1)} %get-tuple-element.6), calls=%async_computation.1 | async-start | bytes 3670016 | tf_op jit(solution)/shard_map/all_to_all | solution.py:373
  119.9 3.8 %slice-start.1 = ((bf16[1,7,64,64]{3,2,1,0:T(8,128)(2,1)}), bf16[1,4,64,64]{3,2,1,0:T(8,128)(2,1)S(1)}, s32[]{:S(2)}) async-start(bf16[1,7,64,64]{3,2,1,0:T(8,128)(2,1)} %param.7), calls=%async_computation.5 | async-start | bytes 131072 | tf_op jit(solution)/shard_map/slice | solution.py:368
Sparse Core Ops, SparseCore 0:
  25.4 52.7 all-gather.4
  80.3 52.4 all-gather.2

commit v5 on v4

--- a/solution.py
+++ b/solution.py
@@ -22,8 +22,10 @@
 REPLICA = ("y_lo", "x")
 RING = ("z", "core")
 PIECES = 8
-VMEM_LIMIT = 48 * 1024 * 1024
+VMEM_LIMIT=24*1024*1024
+SMALL_LIMIT=12*1024*1024
 AHEAD = 3
+NEAR_PIECES = 4
 EARLY_PIECE = 1536
 EARLY_COUNT = 8
 ACROSS = (((1,), (1,)), ((), ()))
@@ -166,8 +168,8 @@
     )(*hidden, weights, targets)
 
 
-def late_kernel(steps, hidden, base, targets, out, held, outs, both_ref, hidden_sem, base_sem,
-                out_sem):
+def late_kernel(steps, hidden, base, targets, near, far, held, outs, both_ref, hidden_sem,
+                base_sem, out_sem):
     rows = hidden.shape[0]
     count, features, width = base.shape
     inverse_root = 1.0 / math.sqrt(hidden.shape[1])
@@ -180,8 +182,7 @@
             base.at[piece], held.at[piece, pl.ds(0, features)], base_sem.at[piece])
 
     def out_copy(piece):
-        return pltpu.make_async_copy(
-            outs.at[piece], out.at[:, pl.ds(piece * width, width)], out_sem.at[piece])
+        return pltpu.make_async_copy(outs.at[piece], far.at[piece], out_sem.at[piece])
 
     def start(piece):
         for copy in copies(piece):
@@ -202,15 +203,17 @@
                      lambda x: x)
     factors = residual.astype(jnp.bfloat16)
 
-    def write(piece, carry):
+    kept = near.shape[0]
+    for piece in [*range(kept, count), *range(kept)]:
         update = (inner_rate * inverse_root) * jnp.dot(
             factors, held[piece, features:], preferred_element_type=jnp.float32)
-        outs[piece] = (held[piece, :features].astype(jnp.float32) - update).astype(jnp.bfloat16)
-        out_copy(piece).start()
-        return carry
-
-    lax.fori_loop(0, count, write, 0, unroll=4)
-    for piece in range(count):
+        result = (held[piece, :features].astype(jnp.float32) - update).astype(jnp.bfloat16)
+        if piece < kept:
+            near[piece] = result
+        else:
+            outs[piece - kept] = result
+            out_copy(piece - kept).start()
+    for piece in range(count - kept):
         out_copy(piece).wait()
 
 
@@ -219,14 +222,18 @@
     count, features, width = base.shape
     anywhere = pl.BlockSpec(memory_space=pl.ANY)
     semaphores = pltpu.SemaphoreType.DMA((count,))
+    far = (count - NEAR_PIECES, features, width)
     return pl.pallas_call(
         functools.partial(late_kernel, steps),
-        out_shape=pltpu.HBM((features, columns), jnp.bfloat16),
+        out_shape=(
+            jax.ShapeDtypeStruct((NEAR_PIECES, features, width), jnp.bfloat16),
+            pltpu.HBM(far, jnp.bfloat16),
+        ),
         in_specs=[anywhere, anywhere, pl.BlockSpec(memory_space=pltpu.VMEM)],
-        out_specs=anywhere,
+        out_specs=(pl.BlockSpec(memory_space=pltpu.VMEM), anywhere),
         scratch_shapes=[
             pltpu.VMEM((count, features + rows, width), jnp.bfloat16),
-            pltpu.VMEM((count, features, width), jnp.bfloat16),
+            pltpu.VMEM(far, jnp.bfloat16),
             pltpu.VMEM((features + rows, rows), jnp.float32),
             semaphores, semaphores, semaphores,
         ],
@@ -290,7 +297,7 @@
             pltpu.SemaphoreType.DMA((OUTER_PARTS, groups)),
             pltpu.SemaphoreType.DMA((2, OUTER_PARTS)),
         ],
-        compiler_params=pltpu.CompilerParams(vmem_limit_bytes=VMEM_LIMIT),
+        compiler_params=pltpu.CompilerParams(vmem_limit_bytes=SMALL_LIMIT),
         cost_estimate=pl.CostEstimate(
             flops=groups * features * width, bytes_accessed=4 * groups * features * width,
             transcendentals=0),
@@ -298,47 +305,52 @@
     )(received, momentum, rows_before)
 
 
-def mix_kernel(late, outer, out, late_part, mixed, late_sem, out_sem):
+def mix_kernel(near, far, outer, out, late_part, mixed, late_sem, out_sem):
     count, _, width = outer.shape
-
-    def columns(piece):
-        return pl.ds(piece * width, width)
-
-    loads, stores = [], []
+    kept = near.shape[0]
+    loads = [
+        pltpu.make_async_copy(far.at[piece], late_part.at[piece], late_sem.at[piece])
+        for piece in range(count - kept)
+    ]
+    for load in loads:
+        load.start()
+    stores = []
     for piece in range(count):
-        loads.append(pltpu.make_async_copy(
-            late.at[:, columns(piece)], late_part.at[piece], late_sem.at[piece]))
+        if piece < kept:
+            late = near[piece]
+        else:
+            loads[piece - kept].wait()
+            late = late_part[piece - kept]
+        mixed[piece] = (
+            mixing * late.astype(jnp.float32) + (1.0 - mixing) * outer[piece].astype(jnp.float32)
+        ).astype(jnp.bfloat16)
         stores.append(pltpu.make_async_copy(
-            mixed.at[piece], out.at[:, columns(piece)], out_sem.at[piece]))
-        loads[-1].start()
-    for piece in range(count):
-        loads[piece].wait()
-        mixed[piece] = (
-            mixing * late_part[piece].astype(jnp.float32)
-            + (1.0 - mixing) * outer[piece].astype(jnp.float32)
-        ).astype(jnp.bfloat16)
-        stores[piece].start()
+            mixed.at[piece], out.at[:, pl.ds(piece * width, width)], out_sem.at[piece]))
+        stores[-1].start()
     for store in stores:
         store.wait()
 
 
-def mix(late, outer):
-    features, columns = late.shape
+def mix(near, far, outer):
+    count, features, width = outer.shape
+    whole = pl.BlockSpec(memory_space=pltpu.VMEM)
     anywhere = pl.BlockSpec(memory_space=pl.ANY)
-    held = pltpu.VMEM(outer.shape, jnp.bfloat16)
-    semaphores = pltpu.SemaphoreType.DMA((PIECES,))
     return pl.pallas_call(
         mix_kernel,
-        out_shape=pltpu.HBM((features, columns), jnp.bfloat16),
-        in_specs=[anywhere, pl.BlockSpec(memory_space=pltpu.VMEM)],
+        out_shape=pltpu.HBM((features, count * width), jnp.bfloat16),
+        in_specs=[whole, anywhere, whole],
         out_specs=anywhere,
-        scratch_shapes=[held] * 2 + [semaphores] * 2,
-        compiler_params=pltpu.CompilerParams(vmem_limit_bytes=VMEM_LIMIT),
+        scratch_shapes=[
+            pltpu.VMEM(far.shape, jnp.bfloat16),
+            pltpu.VMEM(outer.shape, jnp.bfloat16),
+            pltpu.SemaphoreType.DMA((far.shape[0],)),
+            pltpu.SemaphoreType.DMA((count,)),
+        ],
+        compiler_params=pltpu.CompilerParams(vmem_limit_bytes=SMALL_LIMIT),
         cost_estimate=pl.CostEstimate(
-            flops=3 * features * columns, bytes_accessed=6 * features * columns,
-            transcendentals=0),
+            flops=3 * outer.size, bytes_accessed=6 * outer.size, transcendentals=0),
         name="mix",
-    )(late, outer)
+    )(near, far, outer)
 
 
 def in_hbm(x):
@@ -351,7 +363,7 @@
     lanes = lax.axis_size("y")
     depth = lax.axis_size("z")
     cores = lax.axis_size("core")
-    own = hidden.reshape(BEFORE + DURING, PIECES, width)
+    own = lax.optimization_barrier(hidden.reshape(BEFORE + DURING, PIECES, width))
 
     def near_rows(part, steps):
         return lax.all_gather(part.reshape(steps * PIECES, width), "y", axis=0, tiled=True)
@@ -367,7 +379,7 @@
     early_targets = jnp.repeat(target_columns(targets[0, :BEFORE], BEFORE), 2, axis=1)
     late_targets = target_columns(targets[0, BEFORE:], DURING)
 
-    encoded = early_window(BEFORE, [early_hidden], weights, early_targets)
+    encoded = early_window(BEFORE, [in_hbm(early_hidden)], weights, early_targets)
 
     def swap(x):
         return lax.all_to_all(x, REPLICA, split_axis=0, concat_axis=0, tiled=True)
@@ -379,8 +391,8 @@
 
     pieces = weights.reshape(features, PIECES, width).transpose(1, 0, 2).astype(jnp.float32)
     base = (pieces - encoded.astype(jnp.float32)).astype(jnp.bfloat16)
-    late = late_window(DURING, late_hidden, in_hbm(base), late_targets)
-    new_weights = mix(in_hbm(late), outer)[None]
+    near, far = late_window(DURING, in_hbm(late_hidden), in_hbm(base), late_targets)
+    new_weights = mix(near, in_hbm(far), outer)[None]
     return (new_weights, outer_shard, momentum_out)
 
 

time: 153 us -> 153 us (level)
  transfers between devices with their start and end apart: 4 -> 4, of which waited for: 4 -> 4; matrix products, arithmetic and copies ran while one was open for 7% -> 7% of each run, Pallas kernels for 12% -> 11%
where the time goes in v5:
time: 153 us
  waiting for transfers between devices  68.5 us (45%)
  blocking collectives  29.1 us (19%)
  Pallas kernels  19.5 us (13%)
  between operations  14.2 us (9%)
  starting transfers between devices  8.73 us (6%)
  other arithmetic  8.1 us (5%)
  local copies, waits for them, and re-layouts  4.35 us (3%)
    all_gather x1, waiting for transfers between devices, body(): early_hidden = lax.all_gather(early_near, RING, axis=0, tiled=True)  38.4 us
    all_gather x2, blocking collectives, near_rows(): lax.all_gather(part.reshape(steps * PIECES, width), 'y', axis=0, tiled=True)  29.1 us
    all_to_all x2, waiting for transfers between devices, swap(): return lax.all_to_all(x, REPLICA, split_axis=0, concat_axis=0, tiled=True)  25.4 us
    all_to_all x2, starting transfers between devices, swap(): return lax.all_to_all(x, REPLICA, split_axis=0, concat_axis=0, tiled=True)  8.65 us
    pallas_call x1, Pallas kernels, early_window(): pl.pallas_call(functools.partial(early_kernel, steps, len(hidden)), out_s...  7.63 us
    pallas_call x1, Pallas kernels, late_window(): pl.pallas_call(functools.partial(late_kernel, steps), out_shape=(jax.Shap...  7.48 us
    all_gather x1, waiting for transfers between devices, body(): late_hidden = lax.all_gather(late_near, RING, axis=0, tiled=True)  4.66 us
    convert_element_type x1, other arithmetic, body(): base = (pieces - encoded.astype(jnp.float32)).astype(jnp.bfloat16)  4.35 us
  transfers between devices with their start and end apart: 4, of which 4 were waited for; matrix products, arithmetic and copies ran while one was open for 7% of the time, Pallas kernels for 11%

profile of v5, /device:TPU:1, one launch (start us, length us, event | category | flops | bytes accessed | tf_op | source)
XLA Modules:
  0.0 152.5 jit_solution(2454492931632070322)
XLA Ops:
  7.2 0.0 all-gather.5.cloned.1.call-start
  7.2 1.0 copy.18
  8.2 16.1 %all_gather.14 = bf16[96,1792]{1,0:T(8,128)(2,1)S(1)} all-gather(bf16[24,1792]{1,0:T(8,128)(2,1)S(1)} %slice_bitcast_fusion.1), channel_id=1, replica_groups=mesh['z'=8,'y'=4,'core'=2,'y_lo'=2,'x'=4] {'y'}, dimensions={0}, use_global_device_ids=true | all-gather | bytes 430080 | tf_op jit(solution)/shard_map/all_gather | solution.py:369
  24.3 1.0 reshape.37
  25.3 0.0 all-gather.3.cloned.1.call-start
  25.4 13.1 %all_gather.12 = bf16[128,1792]{1,0:T(8,128)(2,1)S(1)} all-gather(bf16[32,1792]{1,0:T(8,128)(2,1)S(1)} %slice_bitcast_fusion), channel_id=1, replica_groups=mesh['z'=8,'y'=4,'core'=2,'y_lo'=2,'x'=4] {'y'}, dimensions={0}, use_global_device_ids=true | all-gather | bytes 573440 | tf_op jit(solution)/shard_map/all_gather | solution.py:369
  38.4 1.0 reshape.35
  39.6 0.1 broadcast_in_dim.6
  39.7 0.1 copy.10.refs_2_
  39.8 38.4 %all-gather.5.cloned.1.call-done.refs_0_ = bf16[384,7168]{1,0:T(8,128)(2,1)} async-done(((bf16[24,7168]{1,0:T(8,128)(2,1)}), bf16[384,7168]{1,0:T(8,128)(2,1)}) %all-gather.5.cloned.1.call-update) | async-done | bytes 5505040 | tf_op jit(solution)/shard_map/all_gather | solution.py:376
  78.2 7.6 %early_window.1 = bf16[8,64,1792]{2,1,0:T(8,128)(2,1)} custom-call(bf16[384,7168]{1,0:T(8,128)(2,1)} %all-gather.5.cloned.1.call-done.refs_0_, bf16[64,14336]{1,0:T(8,128)(2,1)S(1)} %copy-done, bf16[64,384]{1,0:T(8,128)(2,1)S(1)} %copy.10.refs_2_), custom_call_target="tpu_custom_call" | custom-call | flops 3523215360 | bytes 9175040 | tf_op jit(solution)/shard_map/early_window/pallas_call | solution.py:150
  85.8 5.0 %all-to-all-start = ((bf16[8,64,1792]{2,1,0:T(8,128)(2,1)}), bf16[8,64,1792]{2,1,0:T(8,128)(2,1)S(1)}, u32[]{:S(2)}, u32[]{:S(2)}) async-start(bf16[8,64,1792]{2,1,0:T(8,128)(2,1)} %early_window.1), calls=%async_computation | async-start | bytes 3670016 | tf_op jit(solution)/shard_map/all_to_all | solution.py:385
  90.9 1.0 constant_dynamic-slice_fusion.rows_before
  91.8 22.5 %all-to-all-done.received = bf16[8,64,1792]{2,1,0:T(8,128)(2,1)S(1)} async-done(((bf16[8,64,1792]{2,1,0:T(8,128)(2,1)}), bf16[8,64,1792]{2,1,0:T(8,128)(2,1)S(1)}, u32[]{:S(2)}, u32[]{:S(2)}) %all-to-all-start) | async-done | bytes 1835040 | tf_op jit(solution)/shard_map/all_to_all | solution.py:385
  114.4 1.9 %outer_step.1 = (bf16[64,1792]{1,0:T(8,128)(2,1)}, f32[64,1792]{1,0:T(8,128)}, bf16[8,64,1792]{2,1,0:T(8,128)(2,1)}) custom-call(bf16[8,64,1792]{2,1,0:T(8,128)(2,1)S(1)} %all-to-all-done.received, f32[64,1792]{1,0:T(8,128)S(1)} %copy-done.1, bf16[64,1792]{1,0:T(8,128)(2,1)S(1)} %constant_dynamic-slice_fusion.rows_before), custom_call_target="tpu_custom_call" | custom-call | flops 917504 | bytes 3670016 | tf_op jit(solution)/shard_map/outer_step/pallas_call | solution.py:285
  116.3 3.6 %all-to-all-start.1 = ((bf16[8,64,1792]{2,1,0:T(8,128)(2,1)}), bf16[8,64,1792]{2,1,0:T(8,128)(2,1)S(1)}, u32[]{:S(2)}, u32[]{:S(2)}) async-start(bf16[8,64,1792]{2,1,0:T(8,128)(2,1)} %get-tuple-element.10), calls=%async_computation.1 | async-start | bytes 3670016 | tf_op jit(solution)/shard_map/all_to_all | solution.py:385
  119.9 3.7 %convert_element_type.21 = f32[64,14336]{1,0:T(8,128)} convert(bf16[64,14336]{1,0:T(8,128)(2,1)} %refs_1_.1) | non-fusion elementwise | flops 917504 | bytes 5505024 | tf_op jit(solution)/shard_map/convert_element_type | solution.py:392
  123.6 0.1 copy.11
  123.7 0.1 copy.12.targets
  123.8 4.3 %fusion.1.base = bf16[8,64,1792]{2,1,0:T(8,128)(2,1)} fusion(f32[8,8,8,1792]{3,2,1,0:T(8,128)} %bitcast.35, bf16[8,64,1792]{2,1,0:T(8,128)(2,1)} %early_window.1), kind=kLoop, calls=%fused_computation.2 | loop fusion | flops 2752512 | bytes 7340032 | tf_op jit(solution)/shard_map/convert_element_type | solution.py:393
  128.1 4.7 %all-gather.3.cloned.1.call-done.hidden = bf16[256,14336]{1,0:T(8,128)(2,1)} async-done(((bf16[16,14336]{1,0:T(8,128)(2,1)}), bf16[256,14336]{1,0:T(8,128)(2,1)}) %all-gather.3.cloned.1.call-update) | async-done | bytes 7340048 | tf_op jit(solution)/shard_map/all_gather | solution.py:378
  132.8 7.5 %late_window.1 = (bf16[4,64,1792]{2,1,0:T(8,128)(2,1)S(1)}, bf16[4,64,1792]{2,1,0:T(8,128)(2,1)}) custom-call(bf16[256,14336]{1,0:T(8,128)(2,1)} %all-gather.3.cloned.1.call-done.hidden, bf16[8,64,1792]{2,1,0:T(8,128)(2,1)} %fusion.1.base, bf16[64,256]{1,0:T(8,128)(2,1)S(1)} %copy.12.targets), custom_call_target="tpu_custom_call" | custom-call | flops 2818572288 | bytes 11010048 | tf_op jit(solution)/shard_map/late_window/pallas_call | solution.py:226
  140.3 2.9 %all-to-all-done.1.outer = bf16[8,64,1792]{2,1,0:T(8,128)(2,1)S(1)} async-done(((bf16[8,64,1792]{2,1,0:T(8,128)(2,1)}), bf16[8,64,1792]{2,1,0:T(8,128)(2,1)S(1)}, u32[]{:S(2)}, u32[]{:S(2)}) %all-to-all-start.1) | async-done | bytes 1835040 | tf_op jit(solution)/shard_map/all_to_all | solution.py:385
  143.2 2.5 %mix.1 = bf16[64,14336]{1,0:T(8,128)(2,1)} custom-call(bf16[4,64,1792]{2,1,0:T(8,128)(2,1)S(1)} %get-tuple-element.8.near, bf16[4,64,1792]{2,1,0:T(8,128)(2,1)} %get-tuple-element.9.far, bf16[8,64,1792]{2,1,0:T(8,128)(2,1)S(1)} %all-to-all-done.1.outer), custom_call_target="tpu_custom_call" | custom-call | flops 2752512 | bytes 5505024 | tf_op jit(solution)/shard_map/mix/pallas_call | solution.py:338
  (14 shorter events, 0.2 us)
Async XLA Ops:
  7.2 71.0 %all-gather.5.cloned.1.call-start = ((), (), s32[]{:S(2)}) async-start(), calls=%async_computation.3 | async-start | bytes 5849088 | tf_op jit(solution)/shard_map/all_gather | solution.py:376
  8.2 31.3 %slice-start = ((bf16[1,7,64,64]{3,2,1,0:T(8,128)(2,1)}), bf16[1,3,64,64]{3,2,1,0:T(8,128)(2,1)S(1)}, s32[]{:S(2)}) async-start(bf16[1,7,64,64]{3,2,1,0:T(8,128)(2,1)} %param.7), calls=%async_computation.4 | async-start | bytes 98304 | tf_op jit(solution)/shard_map/slice | solution.py:379
  24.3 53.9 %copy-start = (bf16[64,14336]{1,0:T(8,128)(2,1)S(1)}, bf16[64,14336]{1,0:T(8,128)(2,1)}, u32[]{:S(2)}) copy-start(bf16[64,14336]{1,0:T(8,128)(2,1)} %refs_1_.1) | copy-start | bytes 5505028
  25.3 107.5 %all-gather.3.cloned.1.call-start = ((), (), s32[]{:S(2)}) async-start(), calls=%async_computation.2 | async-start | bytes 7798784 | tf_op jit(solution)/shard_map/all_gather | solution.py:378
  85.8 28.6 %copy-start.1 = (f32[64,1792]{1,0:T(8,128)S(1)}, f32[64,1792]{1,0:T(8,128)}, u32[]{:S(2)}) copy-start(f32[64,1792]{1,0:T(8,128)} %momentum.1) | copy-start | bytes 1376260
  85.8 28.5 %all-to-all-start = ((bf16[8,64,1792]{2,1,0:T(8,128)(2,1)}), bf16[8,64,1792]{2,1,0:T(8,128)(2,1)S(1)}, u32[]{:S(2)}, u32[]{:S(2)}) async-start(bf16[8,64,1792]{2,1,0:T(8,128)(2,1)} %early_window.1), calls=%async_computation | async-start | bytes 3670016 | tf_op jit(solution)/shard_map/all_to_all | solution.py:385
  116.3 26.9 %all-to-all-start.1 = ((bf16[8,64,1792]{2,1,0:T(8,128)(2,1)}), bf16[8,64,1792]{2,1,0:T(8,128)(2,1)S(1)}, u32[]{:S(2)}, u32[]{:S(2)}) async-start(bf16[8,64,1792]{2,1,0:T(8,128)(2,1)} %get-tuple-element.10), calls=%async_computation.1 | async-start | bytes 3670016 | tf_op jit(solution)/shard_map/all_to_all | solution.py:385
  119.9 3.8 %slice-start.1 = ((bf16[1,7,64,64]{3,2,1,0:T(8,128)(2,1)}), bf16[1,4,64,64]{3,2,1,0:T(8,128)(2,1)S(1)}, s32[]{:S(2)}) async-start(bf16[1,7,64,64]{3,2,1,0:T(8,128)(2,1)} %param.7), calls=%async_computation.5 | async-start | bytes 131072 | tf_op jit(solution)/shard_map/slice | solution.py:380
Sparse Core Ops, SparseCore 0:
  25.4 52.7 all-gather.4
  80.3 52.4 all-gather.2
